TPU v7x, 32 devices: a whole 2x2x4 slice. The times are simulated.
32 devices in a mesh: sec: 4 (over y, core), gy: 2 (over x), gx: 4 (over z).
Axes of the slice: x: 2, y: 2, z: 4, core: 2. Of those that a mesh axis runs over, the one named last changes fastest.
Arguments:
- sections: bfloat16 [4, 320, 640], P('sec', 'gy', 'gx'), may hold values from -16 to 16
- first_kernel: bfloat16 [32, 9], replicated, may hold values from -2 to 2
- first_bias: bfloat16 [32], replicated, may hold values from -3 to 3
- second_kernel: bfloat16 [32, 288], replicated, may hold values from -0.375 to 0.375
- second_bias: bfloat16 [32], replicated, may hold values from -3 to 3
- coarse: int32 [4, 2], P('sec'), may hold values from -4 to 4
- tissue: int32 [4, 2, 4], P('sec', 'gy', 'gx'), may hold values 0 or 1
Outputs:
- features: bfloat16 [4, 320, 20480], P('sec', 'gy', 'gx')
- flow: float32 [4, 3, 2, 2, 4], P('sec', None, None, 'gy', 'gx')
- displacement: float32 [4, 2, 2, 4], P('sec', None, 'gy', 'gx')
All inputs are finite; a program needn't handle non-finite values. No bound on the sum of `tissue` on one device may be relied on, other than what follows from the above.
Results may differ from a plain program's by a relative error of at most 0.0043.
Values may be sent and summed in bfloat16 or wider, within the bound.
A program may use at most 128 MiB of HBM per device.

v0:
```python
import jax
import jax.numpy as jnp
import numpy as np
from jax import lax
from jax.experimental import pallas as pl
from jax.experimental.pallas import tpu as pltpu
from jax.sharding import PartitionSpec as P

LAGS = 3

LAG_WEIGHTS = (1.0, 0.5, 0.25)
STEP_SIZE = 0.3
PLANE_STIFF = 0.5
SPAN = 16
HALF = 128
BF = jnp.bfloat16
F32 = jnp.float32


def extended(cells, sides, width):
    for axis, dim in sides:
        count = lax.axis_size(axis)
        ends = count - 1
        head = lax.slice_in_dim(cells, 0, width, axis=dim)
        tail = lax.slice_in_dim(cells, cells.shape[dim] - width, cells.shape[dim], axis=dim)
        cells = jnp.concatenate(
            [
                lax.ppermute(tail, axis, [(i, (i + 1) % count) for i in range(ends)]),
                cells,
                lax.ppermute(head, axis, [((i + 1) % count, i) for i in range(ends)]),
            ],
            axis=dim,
        )
    return cells


def shifted(value, axis, by):
    count = lax.axis_size(axis)
    pairs = [(i, i + by) for i in range(count) if 0 <= i + by < count]
    return lax.ppermute(value, axis, pairs)


def make_tables(length, parts):
    ramp = np.arange(length)
    angle = (ramp[:, None] * ramp[None, :] % length) * (2.0 * np.pi / length)
    cos, sin = np.cos(angle), np.sin(angle)
    kept = length // 2 + 1
    first = np.zeros((length, 2 * HALF))
    first[:, :kept] = cos[:, :kept]
    first[:, HALF : HALF + kept] = sin[:, :kept]
    chunk = length // parts
    left, back = [], []
    for q in range(parts):
        rows = slice(q * chunk, (q + 1) * chunk)
        left += [np.concatenate([cos[rows], -sin[rows]], 1), np.concatenate([-sin[rows], -cos[rows]], 1)]
        back += [np.concatenate([cos[:, rows], sin[:, rows]], 0), np.concatenate([-sin[:, rows], cos[:, rows]], 0)]
    times = np.full((kept, 1), 2.0)
    times[0] = times[-1] = 1.0
    last = np.zeros((2 * HALF, length))
    last[:kept] = times * cos[:kept]
    last[HALF : HALF + kept] = -times * sin[:kept]
    return (
        first.astype(np.float32),
        np.concatenate(left, 0).astype(np.float32),
        np.concatenate(back, 1).astype(np.float32),
        last.astype(np.float32),
    )


def silu(values):
    half = 0.5 * values
    return half + half * jnp.tanh(half)


def encode_kernel(
    edge, across, down, band1, band1t, band2, band2t, bias1, bias1t, bias2, bias2t, first, left,
    feat, spec, hid, hidt, rowwise,
):
    length = feat.shape[0]
    wide = across.shape[-1]
    ylo, yhi, xlo, xhi = edge[0], edge[1], edge[2], edge[3]
    lanes = band1.shape[1]
    channels = lanes // SPAN
    shift = channels.bit_length() - 1

    def first_layer(blk, carry):
        r0 = pl.multiple_of(blk * SPAN, SPAN)
        c0 = pl.multiple_of(blk * lanes, lanes)
        rhs = jnp.concatenate([down[a, pl.ds(r0, 2 * SPAN), :] for a in range(3)], axis=0)
        summed = lax.dot_general(rhs, band1[...], (((0,), (0,)), ((), ())), preferred_element_type=F32)
        row = lax.broadcasted_iota(jnp.int32, (wide, 1), 0)
        col = r0 + lax.shift_right_logical(lax.broadcasted_iota(jnp.int32, (1, lanes), 1), shift)
        keep = ((row >= ylo) & (row <= yhi)).astype(F32) * ((col >= xlo) & (col <= xhi)).astype(F32)
        value = silu(summed + bias1[...]) * keep
        for a in range(3):
            hid[a, :, pl.ds(c0, lanes)] = value[a : a + length].astype(BF)

        rhs = jnp.concatenate([across[b, pl.ds(r0, 2 * SPAN), :] for b in range(3)], axis=0)
        summed = jnp.dot(band1t[...], rhs, preferred_element_type=F32)
        row = r0 + lax.shift_right_logical(lax.broadcasted_iota(jnp.int32, (lanes, 1), 0), shift)
        col = lax.broadcasted_iota(jnp.int32, (1, wide), 1)
        keep = ((row >= ylo) & (row <= yhi)).astype(F32) * ((col >= xlo) & (col <= xhi)).astype(F32)
        value = silu(summed + bias1t[...]) * keep
        for b in range(3):
            hidt[b, pl.ds(c0, lanes), :] = value[:, b : b + length].astype(BF)
        return carry

    lax.fori_loop(0, wide // SPAN, first_layer, 0)
    cols = band2.shape[2]
    depth = band2.shape[1]

    def second_layer(blk, carry):
        c0 = pl.multiple_of(blk * cols, cols)
        acc = bias2[...] + jnp.dot(hid[0, :, pl.ds(c0, depth)], band2[0], preferred_element_type=F32)
        for a in range(1, 3):
            acc = acc + jnp.dot(hid[a, :, pl.ds(c0, depth)], band2[a], preferred_element_type=F32)
        feat[:, pl.ds(c0, cols)] = acc.astype(BF)
        acc = bias2t[...] + jnp.dot(band2t[0], hidt[0, pl.ds(c0, depth), :], preferred_element_type=F32)
        for b in range(1, 3):
            acc = acc + jnp.dot(band2t[b], hidt[b, pl.ds(c0, depth), :], preferred_element_type=F32)
        pair = jnp.dot(acc.astype(BF), first[...], preferred_element_type=F32)
        rowwise[0, pl.ds(c0, cols), :] = pair[:, :HALF]
        rowwise[1, pl.ds(c0, cols), :] = pair[:, HALF:]
        return carry

    lax.fori_loop(0, length * channels // cols, second_layer, 0)
    parts = spec.shape[0]
    size = spec.shape[2]

    def columns(step, carry):
        c = step * 2
        both = jnp.concatenate(
            [
                jnp.concatenate(
                    [rowwise[q, pl.ds(c + i, length, stride=channels), :].astype(BF) for q in range(2)],
                    axis=0,
                )
                for i in range(2)
            ],
            axis=1,
        )
        out = jnp.dot(left[...], both, preferred_element_type=F32).astype(BF)
        for q in range(parts):
            for i in range(2):
                spec[q, c + i] = out[q * size : (q + 1) * size, i * HALF : (i + 1) * HALF]
        return carry

    lax.fori_loop(0, channels // 2, columns, 0)


def power_kernel(got, out):
    secs, channels, size, lanes = got.shape
    half = size // 2
    out[...] = jnp.zeros_like(out)

    def channel(c, carry):
        values = [got[t, c].astype(F32) for t in range(secs)]
        for s in range(secs):
            for lag in range(1, min(s, LAGS) + 1):
                cur, ear = values[s], values[s - lag]
                out[s, lag - 1, :half] += ear[:half] * cur[:half] + ear[half:] * cur[half:]
                out[s, lag - 1, half:] += ear[:half] * cur[half:] - ear[half:] * cur[:half]
        return carry

    lax.fori_loop(0, channels, channel, 0)


def peak_kernel(scale, power, back, last, flow):
    parts = power.shape[0]
    length = last.shape[1]
    row = lax.broadcasted_iota(jnp.int32, (length, 1), 0)
    col = lax.broadcasted_iota(jnp.int32, (1, length), 1)
    sign_y = jnp.where(row < length // 2, row, row - length).astype(F32)
    sign_x = jnp.where(col < length // 2, col, col - length).astype(F32)
    place = lax.broadcasted_iota(jnp.int32, flow.shape, 0)
    side = lax.broadcasted_iota(jnp.int32, flow.shape, 1)
    result = jnp.zeros(flow.shape, F32)
    stacked = jnp.concatenate(
        [jnp.concatenate([power[q, lag] for q in range(parts)], axis=0) for lag in range(LAGS)], axis=1
    )
    mixed = jnp.dot(back[...], stacked, precision=lax.Precision.HIGHEST, preferred_element_type=F32)
    for lag in range(LAGS):
        part = mixed[:, lag * HALF : (lag + 1) * HALF]
        lhs = jnp.concatenate([part[:length], part[length:]], axis=1)
        scores = jnp.dot(lhs, last[...], precision=lax.Precision.HIGHEST, preferred_element_type=F32) * scale
        chances = jnp.exp(scores - jnp.max(scores))
        total = jnp.sum(chances)
        flow_y = jnp.sum(chances * sign_y) / total
        flow_x = jnp.sum(chances * sign_x) / total
        result = jnp.where((place == lag) & (side == 0), flow_y, result)
        result = jnp.where((place == lag) & (side == 1), flow_x, result)
    flow[...] = result


def bands(first_kernel, second_kernel):
    channels = first_kernel.shape[0]
    delta = np.arange(2 * SPAN)[:, None] - np.arange(SPAN)[None, :]
    hot1 = jnp.asarray(np.stack([delta == t for t in range(3)]).astype(np.float32), BF)
    taps = first_kernel.reshape(channels, 3, 3)
    band1 = jnp.einsum("txl,kat->axlk", hot1, taps).reshape(6 * SPAN, SPAN * channels)
    band1t = jnp.einsum("tyl,ktb->lkby", hot1, taps).reshape(SPAN * channels, 6 * SPAN)
    short = SPAN // 2
    delta = np.arange(12)[:, None] - np.arange(short)[None, :]
    hot2 = jnp.asarray(np.stack([delta == t for t in range(3)]).astype(np.float32), BF)
    taps = second_kernel.reshape(channels, 3, 3, channels)
    band2 = jnp.einsum("txl,catk->axklc", hot2, taps).reshape(3, 12 * channels, short * channels)
    band2t = jnp.einsum("tyl,ctbk->blcyk", hot2, taps).reshape(3, short * channels, 12 * channels)
    return band1, band1t, band2, band2t


def body(sections, first_kernel, first_bias, second_kernel, second_bias, coarse, tissue):
    length = sections.shape[-1]
    channels = first_kernel.shape[0]
    secs = lax.axis_size("sec")
    first, left, back, last = make_tables(length, secs)
    row_index = lax.axis_index("gy")
    col_index = lax.axis_index("gx")
    rows_count = lax.axis_size("gy")
    cols_count = lax.axis_size("gx")
    sec_index = lax.axis_index("sec")

    band1, band1t, band2, band2t = bands(first_kernel, second_kernel)
    bias1 = jnp.tile(first_bias.astype(F32), SPAN)
    bias2 = jnp.tile(second_bias.astype(F32), SPAN // 2)
    metadata = jnp.concatenate([tissue.reshape(1), coarse.reshape(2)]).astype(BF)
    prior_all = [shifted(metadata, "sec", lag).astype(F32) for lag in range(1, LAGS + 1)]

    wide = length + SPAN
    image = extended(sections, (("gy", 1), ("gx", 2)), 2)[0]
    pad = wide + SPAN + 2 - image.shape[0]
    image = jnp.pad(image, ((0, pad), (0, pad)))
    across = jnp.stack([image[: wide + SPAN, b : b + wide] for b in range(3)])
    turned = image.T
    down = jnp.stack([turned[: wide + SPAN, a : a + wide] for a in range(3)])
    edge = jnp.stack(
        [
            jnp.where(row_index == 0, 1, 0),
            jnp.where(row_index == rows_count - 1, length, length + 1),
            jnp.where(col_index == 0, 1, 0),
            jnp.where(col_index == cols_count - 1, length, length + 1),
        ]
    ).astype(jnp.int32)
    vmem = pl.BlockSpec(memory_space=pltpu.VMEM)
    size = 2 * length // secs
    features, spec = pl.pallas_call(
        encode_kernel,
        out_shape=(
            jax.ShapeDtypeStruct((length, length * channels), BF),
            jax.ShapeDtypeStruct((secs, channels, size, HALF), BF),
        ),
        in_specs=[pl.BlockSpec(memory_space=pltpu.SMEM)] + [vmem] * 12,
        out_specs=(vmem, vmem),
        scratch_shapes=[
            pltpu.VMEM((3, length, wide * channels), BF),
            pltpu.VMEM((3, wide * channels, length), BF),
            pltpu.VMEM((2, length * channels, HALF), F32),
        ],
        compiler_params=pltpu.CompilerParams(vmem_limit_bytes=48 * 1024 * 1024),
        name="encode",
    )(
        edge, across, down, band1, band1t, band2, band2t,
        bias1[None, :], bias1[:, None], bias2[None, :], bias2[:, None],
        jnp.asarray(first, BF), jnp.asarray(left, BF),
    )

    got = lax.all_to_all(spec, "sec", 0, 0)
    power = pl.pallas_call(
        power_kernel,
        out_shape=jax.ShapeDtypeStruct((secs, LAGS, size, HALF), F32),
        in_specs=[vmem],
        out_specs=vmem,
        compiler_params=pltpu.CompilerParams(vmem_limit_bytes=32 * 1024 * 1024),
        name="power",
    )(got)
    power = lax.all_to_all(power, "sec", 0, 0)
    scale = 1.0 / (float(length) ** 3 * channels)
    peaks = pl.pallas_call(
        lambda *refs: peak_kernel(scale, *refs),
        out_shape=jax.ShapeDtypeStruct((8, 128), F32),
        in_specs=[vmem] * 3,
        out_specs=vmem,
        compiler_params=pltpu.CompilerParams(vmem_limit_bytes=32 * 1024 * 1024),
        name="peak",
    )(power, jnp.asarray(back), jnp.asarray(last))
    reach = jnp.arange(1, LAGS + 1, dtype=jnp.int32)
    flows = jnp.where((sec_index >= reach)[:, None], peaks[:LAGS, :2], 0.0)

    own_mask = tissue.reshape(()).astype(F32)
    own = coarse.reshape(2).astype(F32)
    weights = [
        jnp.where(sec_index >= lag, LAG_WEIGHTS[lag - 1] * own_mask * prior_all[lag - 1][0], 0.0)
        for lag in range(1, LAGS + 1)
    ]
    targets = [flows[lag - 1] + own - prior_all[lag - 1][1:] for lag in range(1, LAGS + 1)]
    pulled = jnp.zeros_like(own)
    for lag in range(1, LAGS + 1):
        pulled = pulled + weights[lag - 1] * (prior_all[lag - 1][1:] + targets[lag - 1] - own)
    nodes = own + STEP_SIZE * pulled
    count = (
        (row_index > 0).astype(F32)
        + (row_index < rows_count - 1).astype(F32)
        + (col_index > 0).astype(F32)
        + (col_index < cols_count - 1).astype(F32)
    )
    pulled = jnp.zeros_like(own)
    for lag in range(1, LAGS + 1):
        pulled = pulled + weights[lag - 1] * (shifted(nodes, "sec", lag) + targets[lag - 1] - nodes)
    beside = shifted(nodes, "gy", 1) + shifted(nodes, "gy", -1) + shifted(nodes, "gx", 1) + shifted(nodes, "gx", -1)
    nodes = nodes + STEP_SIZE * (pulled + PLANE_STIFF * (beside - count * nodes))
    return (
        features.reshape(1, length, features.shape[-1]),
        flows.reshape(1, LAGS, 2, 1, 1),
        nodes.reshape(1, 2, 1, 1),
    )


def solution(mesh):
    in_specs = (P("sec", "gy", "gx"), P(), P(), P(), P(), P("sec", None), P("sec", "gy", "gx"))
    out_specs = (P("sec", "gy", "gx"), P("sec", None, None, "gy", "gx"), P("sec", None, "gy", "gx"))
    return jax.shard_map(body, mesh=mesh, in_specs=in_specs, out_specs=out_specs, check_vma=False)
```

profile of v0, /device:TPU:1, one launch (start us, length us, event | category | flops | bytes accessed | tf_op | source)
XLA Modules:
  0.0 139.9 jit_solution(15935407433877637986)
XLA Ops:
  0.6 0.7 fusion.15
  1.5 1.3 collective-permute-start.1
  2.9 4.0 %collective-permute-start = (bf16[1,2,160]{1,2,0:T(8,128)(2,1)S(1)}, bf16[1,2,160]{1,2,0:T(8,128)(2,1)S(1)}, u32[]{:S(2)}, u32[]{:S(2)}) collective-permute-start(bf16[1,2,160]{1,2,0:T(8,128)(2,1)S(1)} %copy.28), channel_id=1, source_target_pairs={{0,4},{1,5},{2,6},{3,7},{8,12},{9,13},{10,14},{11,15},{16,20},{17,... | collective-permute-start | bytes 1928 | tf_op jit(solution)/shard_map/ppermute | solution.py:28
  6.9 0.7 reshape.64
  7.6 0.7 reshape.50
  8.3 0.8 reshape.67
  9.2 0.9 reshape.53
  10.1 1.0 convolution_bitcast_fusion.3
  11.1 1.0 convolution_bitcast_fusion.2
  12.2 3.2 %convolution_bitcast_fusion.1 = bf16[3,12,32,8,32]{2,1,0,4,3:T(8,128)(2,1)} fusion(bf16[3,12,8,1,1]{1,0,4,3,2:T(4,128)(2,1)} %constant.60, bf16[32,3,3,32,1]{3,2,1,0,4:T(4,128)(2,1)S(1)} %reshape.67), kind=kOutput, calls=%fused_computation.1 | convolution fusion | flops 1769472 | bytes 608832 | tf_op jit(solution)/shard_map/txl,catk->axklc/dot_general | solution.py:206
  15.4 2.5 %convolution_bitcast_fusion = bf16[3,8,32,12,32]{4,3,0,2,1:T(8,128)(2,1)} fusion(bf16[3,12,8,1,1]{1,0,4,3,2:T(4,128)(2,1)S(1)} %copy-done.6, bf16[32,3,3,32]{3,2,1,0:T(4,128)(2,1)S(1)} %reshape.53), kind=kOutput, calls=%fused_computation | convolution fusion | flops 1769472 | bytes 608832 | tf_op jit(solution)/shard_map/tyl,ctbk->blcyk/dot_general | solution.py:207
  18.5 1.3 collective-permute-start.3
  19.8 4.7 %collective-permute-start.2 = (bf16[1,164,2]{1,2,0:T(2,128)(2,1)S(1)}, bf16[1,164,2]{1,2,0:T(2,128)(2,1)S(1)}, u32[]{:S(2)}, u32[]{:S(2)}) collective-permute-start(bf16[1,164,2]{1,2,0:T(2,128)(2,1)S(1)} %get-tuple-element.13), channel_id=1, source_target_pairs={{0,1},{1,2},{2,3},{4,5},{5,6},{6,7},{8,9},{9,10},{10,11},{12,13},{... | collective-permute-start | bytes 1976 | tf_op jit(solution)/shard_map/ppermute | solution.py:28
  25.8 4.8 %reshape.72 = bf16[3,384,256]{1,0,2:T(4,128)(2,1)S(1)} reshape(bf16[3,12,32,8,32]{2,1,0,4,3:T(8,128)(2,1)} %convolution_bitcast_fusion.1) | data formatting | bytes 1179648 | tf_op jit(solution)/shard_map/reshape | solution.py:206
  31.2 4.8 %reshape.73 = bf16[3,256,384]{2,0,1:T(4,128)(2,1)S(1)} reshape(bf16[3,8,32,12,32]{4,3,0,2,1:T(8,128)(2,1)} %convolution_bitcast_fusion) | data formatting | bytes 1179648 | tf_op jit(solution)/shard_map/reshape | solution.py:207
  37.1 29.0 %encode.1 = (bf16[160,5120]{1,0:T(8,128)(2,1)}, bf16[4,32,80,128]{3,2,1,0:T(8,128)(2,1)S(1)}) custom-call(s32[4]{0:T(128)S(1)} %pad_add_fusion.edge, bf16[3,192,176]{2,1,0:T(8,128)(2,1)S(1)} %copy.37.across, bf16[3,192,176]{2,1,0:T(8,128)(2,1)S(1)} %pad_maximum_fusion.down, bf16[96,512]{1,0:T(8,128)(2,1)S(1)} %reshape.51.band1, ...), custom_call_target="tpu_custom_call" | custom-call | tf_op jit(solution)/shard_map/encode/pallas_call | solution.py:245
  66.0 1.5 %copy-done = bf16[4,32,80,128]{3,2,1,0:T(8,128)(2,1)} copy-done((bf16[4,32,80,128]{3,2,1,0:T(8,128)(2,1)}, bf16[4,32,80,128]{3,2,1,0:T(8,128)(2,1)S(1)}, u32[]{:S(2)}) %copy-start) | copy-done | bytes 2621464
  67.5 5.1 %all-to-all-start = ((bf16[4,32,80,128]{3,2,1,0:T(8,128)(2,1)}), bf16[4,32,80,128]{3,2,1,0:T(8,128)(2,1)S(1)}, u32[]{:S(2)}, u32[]{:S(2)}) async-start(bf16[4,32,80,128]{3,2,1,0:T(8,128)(2,1)} %copy-done), calls=%async_computation | async-start | bytes 5242880 | tf_op jit(solution)/shard_map/all_to_all | solution.py:266
  73.4 29.7 %all-to-all-done.got = bf16[4,32,80,128]{3,2,1,0:T(8,128)(2,1)S(1)} async-done(((bf16[4,32,80,128]{3,2,1,0:T(8,128)(2,1)}), bf16[4,32,80,128]{3,2,1,0:T(8,128)(2,1)S(1)}, u32[]{:S(2)}, u32[]{:S(2)}) %all-to-all-start) | async-done | bytes 2621472 | tf_op jit(solution)/shard_map/all_to_all | solution.py:266
  103.1 2.2 %power.1 = f32[4,3,80,128]{3,2,1,0:T(8,128)} custom-call(bf16[4,32,80,128]{3,2,1,0:T(8,128)(2,1)S(1)} %all-to-all-done.got), custom_call_target="tpu_custom_call" | custom-call | tf_op jit(solution)/shard_map/power/pallas_call | solution.py:267
  105.3 4.3 %all-to-all-start.1 = ((f32[4,3,80,128]{3,2,1,0:T(8,128)}), f32[4,3,80,128]{3,2,1,0:T(8,128)S(1)}, u32[]{:S(2)}, u32[]{:S(2)}) async-start(f32[4,3,80,128]{3,2,1,0:T(8,128)} %power.1), calls=%async_computation.1 | async-start | bytes 983040 | tf_op jit(solution)/shard_map/all_to_all | solution.py:275
  110.4 3.9 %collective-permute-start.5 = (bf16[3]{0:T(256)(128)(2,1)S(1)}, bf16[3]{0:T(256)(128)(2,1)S(1)}, u32[]{:S(2)}, u32[]{:S(2)}) collective-permute-start(bf16[3]{0:T(256)(128)(2,1)S(1)} %pad_maximum_fusion.5), channel_id=1, source_target_pairs={{0,16},{8,24},{1,17},{9,25},{2,18},{10,26},{3,19},{11,27},{4,20},{... | collective-permute-start | bytes 26 | tf_op jit(solution)/shard_map/ppermute | solution.py:40
  114.3 1.9 %collective-permute-start.4 = (bf16[3]{0:T(256)(128)(2,1)S(1)}, bf16[3]{0:T(256)(128)(2,1)S(1)}, u32[]{:S(2)}, u32[]{:S(2)}) collective-permute-start(bf16[3]{0:T(256)(128)(2,1)S(1)} %pad_maximum_fusion.5), channel_id=1, source_target_pairs={{0,8},{8,16},{16,24},{1,9},{9,17},{17,25},{2,10},{10,18},{18,26},{... | collective-permute-start | bytes 26 | tf_op jit(solution)/shard_map/ppermute | solution.py:40
  116.3 1.0 collective-permute-done.4
  120.9 2.3 %peak.1 = f32[8,128]{1,0:T(8,128)S(1)} custom-call(f32[4,3,80,128]{3,2,1,0:T(8,128)S(1)} %all-to-all-done.1.refs_0_, f32[320,320]{1,0:T(8,128)S(1)} %copy-done.1, f32[256,160]{1,0:T(8,128)S(1)} %copy-done.2), custom_call_target="tpu_custom_call" | custom-call | tf_op jit(solution)/shard_map/peak/pallas_call | solution.py:277
  123.5 1.3 collective-permute-start.13
  124.8 4.3 %collective-permute-start.12 = (f32[2]{0:T(128)S(1)}, f32[2]{0:T(128)S(1)}, u32[]{:S(2)}, u32[]{:S(2)}) collective-permute-start(f32[2]{0:T(128)S(1)} %bitcast_add_fusion.3), channel_id=1, source_target_pairs={{0,1},{1,2},{2,3},{4,5},{5,6},{6,7},{8,9},{9,10},{10,11},{12,13},{... | collective-permute-start | bytes 32 | tf_op jit(solution)/shard_map/ppermute | solution.py:40
  129.1 1.3 collective-permute-start.10
  130.4 1.3 collective-permute-start.11
  133.0 1.9 %collective-permute-start.8 = (f32[2]{0:T(128)S(1)}, f32[2]{0:T(128)S(1)}, u32[]{:S(2)}, u32[]{:S(2)}) collective-permute-start(f32[2]{0:T(128)S(1)} %bitcast_add_fusion.3), channel_id=1, source_target_pairs={{0,16},{8,24},{1,17},{9,25},{2,18},{10,26},{3,19},{11,27},{4,20},{... | collective-permute-start | bytes 32 | tf_op jit(solution)/shard_map/ppermute | solution.py:40
  134.9 3.4 %collective-permute-start.7 = (f32[2]{0:T(128)S(1)}, f32[2]{0:T(128)S(1)}, u32[]{:S(2)}, u32[]{:S(2)}) collective-permute-start(f32[2]{0:T(128)S(1)} %bitcast_add_fusion.3), channel_id=1, source_target_pairs={{0,8},{8,16},{16,24},{1,9},{9,17},{17,25},{2,10},{10,18},{18,26},{... | collective-permute-start | bytes 32 | tf_op jit(solution)/shard_map/ppermute | solution.py:40
  138.4 0.9 collective-permute-done.7
  (72 shorter events, 8.1 us)
Async XLA Ops:
  0.6 14.8 %copy-start.6 = (bf16[3,12,8,1,1]{1,0,4,3,2:T(4,128)(2,1)S(1)}, bf16[3,12,8,1,1]{1,0,4,3,2:T(4,128)(2,1)}, u32[]{:S(2)}) copy-start(bf16[3,12,8,1,1]{1,0,4,3,2:T(4,128)(2,1)} %constant.60) | copy-start | bytes 1732
  1.5 16.9 %collective-permute-start.1 = (bf16[1,2,160]{1,2,0:T(8,128)(2,1)S(1)}, bf16[1,2,160]{1,2,0:T(8,128)(2,1)S(1)}, u32[]{:S(2)}, u32[]{:S(2)}) collective-permute-start(bf16[1,2,160]{1,2,0:T(8,128)(2,1)S(1)} %copy.29), channel_id=1, source_target_pairs={{4,0},{5,1},{6,2},{7,3},{12,8},{13,9},{14,10},{15,11},{20,16},{21,... | collective-permute-start | bytes 1928 | tf_op jit(solution)/shard_map/ppermute | solution.py:30
  2.9 15.5 %collective-permute-start = (bf16[1,2,160]{1,2,0:T(8,128)(2,1)S(1)}, bf16[1,2,160]{1,2,0:T(8,128)(2,1)S(1)}, u32[]{:S(2)}, u32[]{:S(2)}) collective-permute-start(bf16[1,2,160]{1,2,0:T(8,128)(2,1)S(1)} %copy.28), channel_id=1, source_target_pairs={{0,4},{1,5},{2,6},{3,7},{8,12},{9,13},{10,14},{11,15},{16,20},{17,... | collective-permute-start | bytes 1928 | tf_op jit(solution)/shard_map/ppermute | solution.py:28
  12.2 5.8 %copy-start.5 = (bf16[1,160,160]{2,1,0:T(8,128)(2,1)S(1)}, bf16[1,160,160]{2,1,0:T(8,128)(2,1)}, u32[]{:S(2)}) copy-start(bf16[1,160,160]{2,1,0:T(8,128)(2,1)} %param.13) | copy-start | bytes 153604
  12.2 5.9 %copy-start.8 = (bf16[32]{0:T(256)(128)(2,1)S(1)}, bf16[32]{0:T(256)(128)(2,1)}, u32[]{:S(2)}) copy-start(bf16[32]{0:T(256)(128)(2,1)} %param.15) | copy-start | bytes 196
  12.2 12.3 %copy-start.9 = (bf16[32]{0:T(256)(128)(2,1)S(1)}, bf16[32]{0:T(256)(128)(2,1)}, u32[]{:S(2)}) copy-start(bf16[32]{0:T(256)(128)(2,1)} %param.17) | copy-start | bytes 196
  18.5 17.6 %collective-permute-start.3 = (bf16[1,164,2]{1,2,0:T(2,128)(2,1)S(1)}, bf16[1,164,2]{1,2,0:T(2,128)(2,1)S(1)}, u32[]{:S(2)}, u32[]{:S(2)}) collective-permute-start(bf16[1,164,2]{1,2,0:T(2,128)(2,1)S(1)} %get-tuple-element.14), channel_id=1, source_target_pairs={{1,0},{2,1},{3,2},{5,4},{6,5},{7,6},{9,8},{10,9},{11,10},{13,12},{... | collective-permute-start | bytes 1976 | tf_op jit(solution)/shard_map/ppermute | solution.py:30
  19.8 16.3 %collective-permute-start.2 = (bf16[1,164,2]{1,2,0:T(2,128)(2,1)S(1)}, bf16[1,164,2]{1,2,0:T(2,128)(2,1)S(1)}, u32[]{:S(2)}, u32[]{:S(2)}) collective-permute-start(bf16[1,164,2]{1,2,0:T(2,128)(2,1)S(1)} %get-tuple-element.13), channel_id=1, source_target_pairs={{0,1},{1,2},{2,3},{4,5},{5,6},{6,7},{8,9},{9,10},{10,11},{12,13},{... | collective-permute-start | bytes 1976 | tf_op jit(solution)/shard_map/ppermute | solution.py:28
  36.0 0.9 copy-start.3
  36.0 1.0 copy-start.4
  66.0 1.5 %copy-start = (bf16[4,32,80,128]{3,2,1,0:T(8,128)(2,1)}, bf16[4,32,80,128]{3,2,1,0:T(8,128)(2,1)S(1)}, u32[]{:S(2)}) copy-start(bf16[4,32,80,128]{3,2,1,0:T(8,128)(2,1)S(1)} %get-tuple-element.6) | copy-start | bytes 7864324
  67.5 35.6 %all-to-all-start = ((bf16[4,32,80,128]{3,2,1,0:T(8,128)(2,1)}), bf16[4,32,80,128]{3,2,1,0:T(8,128)(2,1)S(1)}, u32[]{:S(2)}, u32[]{:S(2)}) async-start(bf16[4,32,80,128]{3,2,1,0:T(8,128)(2,1)} %copy-done), calls=%async_computation | async-start | bytes 5242880 | tf_op jit(solution)/shard_map/all_to_all | solution.py:266
  72.7 37.0 %copy-start.7 = (s32[1,2]{1,0:T(1,128)S(1)}, s32[1,2]{1,0:T(1,128)}, u32[]{:S(2)}) copy-start(s32[1,2]{1,0:T(1,128)} %param.18) | copy-start | bytes 28
  72.7 48.2 %copy-start.1 = (f32[320,320]{1,0:T(8,128)S(1)}, f32[320,320]{1,0:T(8,128)}, u32[]{:S(2)}) copy-start(f32[320,320]{1,0:T(8,128)} %constant.52.clone.refs_1_) | copy-start | bytes 1228804
  72.7 48.2 %copy-start.2 = (f32[256,160]{1,0:T(8,128)S(1)}, f32[256,160]{1,0:T(8,128)}, u32[]{:S(2)}) copy-start(f32[256,160]{1,0:T(8,128)} %constant.53.clone.refs_2_) | copy-start | bytes 491524
  105.3 15.6 %all-to-all-start.1 = ((f32[4,3,80,128]{3,2,1,0:T(8,128)}), f32[4,3,80,128]{3,2,1,0:T(8,128)S(1)}, u32[]{:S(2)}, u32[]{:S(2)}) async-start(f32[4,3,80,128]{3,2,1,0:T(8,128)} %power.1), calls=%async_computation.1 | async-start | bytes 983040 | tf_op jit(solution)/shard_map/all_to_all | solution.py:275
  109.7 8.8 %collective-permute-start.6 = (bf16[3]{0:T(256)(128)(2,1)S(1)}, bf16[3]{0:T(256)(128)(2,1)S(1)}, u32[]{:S(2)}, u32[]{:S(2)}) collective-permute-start(bf16[3]{0:T(256)(128)(2,1)S(1)} %pad_maximum_fusion.5), channel_id=1, source_target_pairs={{0,24},{1,25},{2,26},{3,27},{4,28},{5,29},{6,30},{7,31}} | collective-permute-start | bytes 26 | tf_op jit(solution)/shard_map/ppermute | solution.py:40
  110.4 9.3 %collective-permute-start.5 = (bf16[3]{0:T(256)(128)(2,1)S(1)}, bf16[3]{0:T(256)(128)(2,1)S(1)}, u32[]{:S(2)}, u32[]{:S(2)}) collective-permute-start(bf16[3]{0:T(256)(128)(2,1)S(1)} %pad_maximum_fusion.5), channel_id=1, source_target_pairs={{0,16},{8,24},{1,17},{9,25},{2,18},{10,26},{3,19},{11,27},{4,20},{... | collective-permute-start | bytes 26 | tf_op jit(solution)/shard_map/ppermute | solution.py:40
  114.3 3.0 %collective-permute-start.4 = (bf16[3]{0:T(256)(128)(2,1)S(1)}, bf16[3]{0:T(256)(128)(2,1)S(1)}, u32[]{:S(2)}, u32[]{:S(2)}) collective-permute-start(bf16[3]{0:T(256)(128)(2,1)S(1)} %pad_maximum_fusion.5), channel_id=1, source_target_pairs={{0,8},{8,16},{16,24},{1,9},{9,17},{17,25},{2,10},{10,18},{18,26},{... | collective-permute-start | bytes 26 | tf_op jit(solution)/shard_map/ppermute | solution.py:40
  123.5 9.5 %collective-permute-start.13 = (f32[2]{0:T(128)S(1)}, f32[2]{0:T(128)S(1)}, u32[]{:S(2)}, u32[]{:S(2)}) collective-permute-start(f32[2]{0:T(128)S(1)} %bitcast_add_fusion.3), channel_id=1, source_target_pairs={{1,0},{2,1},{3,2},{5,4},{6,5},{7,6},{9,8},{10,9},{11,10},{13,12},{... | collective-permute-start | bytes 32 | tf_op jit(solution)/shard_map/ppermute | solution.py:40
  124.8 10.1 %collective-permute-start.12 = (f32[2]{0:T(128)S(1)}, f32[2]{0:T(128)S(1)}, u32[]{:S(2)}, u32[]{:S(2)}) collective-permute-start(f32[2]{0:T(128)S(1)} %bitcast_add_fusion.3), channel_id=1, source_target_pairs={{0,1},{1,2},{2,3},{4,5},{5,6},{6,7},{8,9},{9,10},{10,11},{12,13},{... | collective-permute-start | bytes 32 | tf_op jit(solution)/shard_map/ppermute | solution.py:40
  129.1 9.3 %collective-permute-start.10 = (f32[2]{0:T(128)S(1)}, f32[2]{0:T(128)S(1)}, u32[]{:S(2)}, u32[]{:S(2)}) collective-permute-start(f32[2]{0:T(128)S(1)} %bitcast_add_fusion.3), channel_id=1, source_target_pairs={{0,4},{1,5},{2,6},{3,7},{8,12},{9,13},{10,14},{11,15},{16,20},{17,... | collective-permute-start | bytes 32 | tf_op jit(solution)/shard_map/ppermute | solution.py:40
  130.4 8.0 %collective-permute-start.11 = (f32[2]{0:T(128)S(1)}, f32[2]{0:T(128)S(1)}, u32[]{:S(2)}, u32[]{:S(2)}) collective-permute-start(f32[2]{0:T(128)S(1)} %bitcast_add_fusion.3), channel_id=1, source_target_pairs={{4,0},{5,1},{6,2},{7,3},{12,8},{13,9},{14,10},{15,11},{20,16},{21,... | collective-permute-start | bytes 32 | tf_op jit(solution)/shard_map/ppermute | solution.py:40
  131.7 6.7 %collective-permute-start.9 = (f32[2]{0:T(128)S(1)}, f32[2]{0:T(128)S(1)}, u32[]{:S(2)}, u32[]{:S(2)}) collective-permute-start(f32[2]{0:T(128)S(1)} %bitcast_add_fusion.3), channel_id=1, source_target_pairs={{0,24},{1,25},{2,26},{3,27},{4,28},{5,29},{6,30},{7,31}} | collective-permute-start | bytes 32 | tf_op jit(solution)/shard_map/ppermute | solution.py:40
  133.0 5.4 %collective-permute-start.8 = (f32[2]{0:T(128)S(1)}, f32[2]{0:T(128)S(1)}, u32[]{:S(2)}, u32[]{:S(2)}) collective-permute-start(f32[2]{0:T(128)S(1)} %bitcast_add_fusion.3), channel_id=1, source_target_pairs={{0,16},{8,24},{1,17},{9,25},{2,18},{10,26},{3,19},{11,27},{4,20},{... | collective-permute-start | bytes 32 | tf_op jit(solution)/shard_map/ppermute | solution.py:40
  134.9 4.4 %collective-permute-start.7 = (f32[2]{0:T(128)S(1)}, f32[2]{0:T(128)S(1)}, u32[]{:S(2)}, u32[]{:S(2)}) collective-permute-start(f32[2]{0:T(128)S(1)} %bitcast_add_fusion.3), channel_id=1, source_target_pairs={{0,8},{8,16},{16,24},{1,9},{9,17},{17,25},{2,10},{10,18},{18,26},{... | collective-permute-start | bytes 32 | tf_op jit(solution)/shard_map/ppermute | solution.py:40
where the time goes:
time: 142 us; the launch traced here: 140 us
  starting transfers between devices  41.3 us (29%)
  Pallas kernels  33.5 us (24%)
  waiting for transfers between devices  31.7 us (22%)
  local copies, waits for them, and re-layouts  20.4 us (14%)
  matrix products  7.75 us (5%)
  between operations  3.91 us (3%)
    all_to_all x1, waiting for transfers between devices, body(): got = lax.all_to_all(spec, 'sec', 0, 0)  29.7 us
    pallas_call x1, Pallas kernels, body(): pl.pallas_call(encode_kernel, out_shape=(jax.ShapeDtypeStruct((length, le...  29 us
    ppermute x10, starting transfers between devices, shifted(): return lax.ppermute(value, axis, pairs)  20.6 us
    ppermute x2, starting transfers between devices, extended(): lax.ppermute(tail, axis, [(i, (i + 1) % count) for i in range(ends)])  8.64 us
    reshape x2, local copies, waits for them, and re-layouts, bands(): jnp.einsum('txl,catk->axklc', hot2, taps)  5.43 us
    all_to_all x1, starting transfers between devices, body(): got = lax.all_to_all(spec, 'sec', 0, 0)  5.13 us
    reshape x2, local copies, waits for them, and re-layouts, bands(): jnp.einsum('tyl,ctbk->blcyk', hot2, taps)  4.89 us
    all_to_all x1, starting transfers between devices, body(): power = lax.all_to_all(power, 'sec', 0, 0)  4.31 us
  transfers between devices with their start and end apart: 16, of which 3 were waited for; matrix products, arithmetic and copies ran while one was open for 18% of the time, Pallas kernels for 0%

commit v1 on v0

v1 whole, which is shorter than its diff:
```python
import functools

import jax
import jax.numpy as jnp
import numpy as np
from jax import lax
from jax.experimental import pallas as pl
from jax.experimental.pallas import tpu as pltpu
from jax.sharding import PartitionSpec as P

LAGS = 3

LAG_WEIGHTS = (1.0, 0.5, 0.25)
STEP_SIZE = 0.3
PLANE_STIFF = 0.5
SPAN = 16
HALF = 128
BF = jnp.bfloat16
F32 = jnp.float32


def extended(cells, sides, width):
    for axis, dim in sides:
        count = lax.axis_size(axis)
        ends = count - 1
        head = lax.slice_in_dim(cells, 0, width, axis=dim)
        tail = lax.slice_in_dim(cells, cells.shape[dim] - width, cells.shape[dim], axis=dim)
        cells = jnp.concatenate(
            [
                lax.ppermute(tail, axis, [(i, (i + 1) % count) for i in range(ends)]),
                cells,
                lax.ppermute(head, axis, [((i + 1) % count, i) for i in range(ends)]),
            ],
            axis=dim,
        )
    return cells


def make_tables(length, parts):
    ramp = np.arange(length)
    angle = (ramp[:, None] * ramp[None, :] % length) * (2.0 * np.pi / length)
    cos, sin = np.cos(angle), np.sin(angle)
    kept = length // 2 + 1
    first = np.zeros((length, 2 * HALF))
    first[:, :kept] = cos[:, :kept]
    first[:, HALF : HALF + kept] = sin[:, :kept]
    chunk = length // parts
    left, back = [], []
    for q in range(parts):
        rows = slice(q * chunk, (q + 1) * chunk)
        left += [np.concatenate([cos[rows], -sin[rows]], 1), np.concatenate([-sin[rows], -cos[rows]], 1)]
        back += [np.concatenate([cos[:, rows], sin[:, rows]], 0), np.concatenate([-sin[:, rows], cos[:, rows]], 0)]
    times = np.full((kept, 1), 2.0)
    times[0] = times[-1] = 1.0
    last = np.zeros((2 * HALF, length))
    last[:kept] = times * cos[:kept]
    last[HALF : HALF + kept] = -times * sin[:kept]
    return (
        first.astype(np.float32),
        np.concatenate(left, 0).astype(np.float32),
        np.concatenate(back, 1).astype(np.float32),
        last.astype(np.float32),
    )


def silu(values):
    half = 0.5 * values
    return half + half * jnp.tanh(half)


def tiled_eye(channels, lanes):
    lane = lax.broadcasted_iota(jnp.int32, (channels, lanes), 1)
    row = lax.broadcasted_iota(jnp.int32, (channels, lanes), 0)
    return ((lane & (channels - 1)) == row).astype(F32)


def across_rows(left, right):
    return lax.dot_general(left, right, (((0,), (0,)), ((), ())), preferred_element_type=F32)


def encode_kernel(
    across, down, kernel1, kernel2, bias1_in, bias2_in, first,
    feat, rowwise, hid, hidt, band1, band1t, band2, band2t, bias1, bias1t, bias2, bias2t,
):
    length = feat.shape[0]
    wide = across.shape[-1]
    lanes = band1.shape[1]
    cols = band2.shape[2]
    depth = band2.shape[1]
    channels = lanes // SPAN
    shift = channels.bit_length() - 1
    row_index, col_index = lax.axis_index("gy"), lax.axis_index("gx")
    ylo = jnp.where(row_index == 0, 1, 0)
    yhi = jnp.where(row_index == lax.axis_size("gy") - 1, length, length + 1)
    xlo = jnp.where(col_index == 0, 1, 0)
    xhi = jnp.where(col_index == lax.axis_size("gx") - 1, length, length + 1)

    eye = tiled_eye(channels, lanes)
    eye_bf = eye.astype(BF)
    for source, row_ref, col_ref, width in ((bias1_in, bias1, bias1t, lanes), (bias2_in, bias2, bias2t, cols)):
        spread = jnp.broadcast_to(source[...].astype(F32), (8, channels)).astype(BF)
        row = jnp.dot(spread, eye_bf[:, :width], preferred_element_type=F32)
        row_ref[...] = row
        col_ref[...] = jnp.transpose(jnp.broadcast_to(row[0:1], (128, width)))
    tap1 = across_rows(kernel1[...], eye_bf)
    unit = lax.shift_right_logical(lax.broadcasted_iota(jnp.int32, (2 * SPAN, lanes), 1), shift)
    gap = lax.broadcasted_iota(jnp.int32, (2 * SPAN, lanes), 0) - unit
    for ref, outer, inner in ((band1, 3, 1), (band1t, 1, 3)):
        parts = []
        for p in range(3):
            part = jnp.zeros((2 * SPAN, lanes), F32)
            for q in range(3):
                tap = outer * p + inner * q
                part = jnp.where(gap == q, tap1[tap : tap + 1], part)
            parts.append(part)
        whole = jnp.concatenate(parts, axis=0)
        if outer == 1:
            whole = jnp.transpose(whole)
        ref[...] = whole.astype(BF)
    tap2 = across_rows(kernel2[...], eye_bf[:, :cols])
    unit = lax.shift_right_logical(lax.broadcasted_iota(jnp.int32, (channels, cols), 1), shift)
    for a in range(3):
        for x in range(depth // channels):
            part = jnp.zeros((channels, cols), F32)
            for b in range(3):
                row = (3 * a + b) * channels
                part = jnp.where(unit == x - b, tap2[row : row + channels], part)
            band2[a, x * channels : (x + 1) * channels, :] = part.astype(BF)
    unit = lax.shift_right_logical(lax.broadcasted_iota(jnp.int32, (channels, depth), 1), shift)
    for b in range(3):
        taps = []
        for a in range(3):
            at = (3 * a + b) * channels
            taps.append(jnp.dot(kernel2[:, at : at + channels], eye_bf[:, :depth], preferred_element_type=F32))
        for y in range(cols // channels):
            part = jnp.zeros((channels, depth), F32)
            for a in range(3):
                part = jnp.where(unit == y + a, taps[a], part)
            band2t[b, y * channels : (y + 1) * channels, :] = part.astype(BF)

    def first_layer(blk, carry):
        r0 = pl.multiple_of(blk * SPAN, SPAN)
        c0 = pl.multiple_of(blk * lanes, lanes)
        rhs = jnp.concatenate([down[a, pl.ds(r0, 2 * SPAN), :] for a in range(3)], axis=0)
        summed = across_rows(rhs, band1[...])
        row = lax.broadcasted_iota(jnp.int32, (wide, 1), 0)
        col = r0 + lax.shift_right_logical(lax.broadcasted_iota(jnp.int32, (1, lanes), 1), shift)
        keep = ((row >= ylo) & (row <= yhi)).astype(F32) * ((col >= xlo) & (col <= xhi)).astype(F32)
        value = silu(summed + bias1[0:1]) * keep
        for a in range(3):
            hid[a, :, pl.ds(c0, lanes)] = value[a : a + length].astype(BF)

        rhs = jnp.concatenate([across[b, pl.ds(r0, 2 * SPAN), :] for b in range(3)], axis=0)
        summed = jnp.dot(band1t[...], rhs, preferred_element_type=F32)
        row = r0 + lax.shift_right_logical(lax.broadcasted_iota(jnp.int32, (lanes, 1), 0), shift)
        col = lax.broadcasted_iota(jnp.int32, (1, wide), 1)
        keep = ((row >= ylo) & (row <= yhi)).astype(F32) * ((col >= xlo) & (col <= xhi)).astype(F32)
        value = silu(summed + bias1t[:, 0:1]) * keep
        for b in range(3):
            hidt[b, pl.ds(c0, lanes), :] = value[:, b : b + length].astype(BF)
        return carry

    lax.fori_loop(0, wide // SPAN, first_layer, 0)

    def second_layer(blk, carry):
        c0 = pl.multiple_of(blk * cols, cols)
        acc = bias2[0:1] + jnp.dot(hid[0, :, pl.ds(c0, depth)], band2[0], preferred_element_type=F32)
        for a in range(1, 3):
            acc = acc + jnp.dot(hid[a, :, pl.ds(c0, depth)], band2[a], preferred_element_type=F32)
        feat[:, pl.ds(c0, cols)] = acc.astype(BF)
        acc = bias2t[:, 0:1] + jnp.dot(band2t[0], hidt[0, pl.ds(c0, depth), :], preferred_element_type=F32)
        for b in range(1, 3):
            acc = acc + jnp.dot(band2t[b], hidt[b, pl.ds(c0, depth), :], preferred_element_type=F32)
        pair = jnp.dot(acc.astype(BF), first[...], preferred_element_type=F32)
        rowwise[0, pl.ds(c0, cols), :] = pair[:, :HALF]
        rowwise[1, pl.ds(c0, cols), :] = pair[:, HALF:]
        return carry

    lax.fori_loop(0, length * channels // cols, second_layer, 0)


def mesh_kernel(
    channels, tissue, coarse, rowwise, left, back, last, flow, nodes_out,
    spec, got, acc, owed, power, node, beside,
    send1, recv1, send2, recv2, send3, recv3,
):
    me = lax.axis_index("sec")
    secs = lax.axis_size("sec")
    row_index, rows_count = lax.axis_index("gy"), lax.axis_size("gy")
    col_index, cols_count = lax.axis_index("gx"), lax.axis_size("gx")
    length = last.shape[1]
    kept = length // 2 + 1
    groups, size = spec.shape[1], spec.shape[2]
    half = size // 2
    peers = [lax.rem(me + r, secs) for r in range(1, secs)]
    targets = [{"sec": peer} for peer in peers]
    targets += [{"gy": lax.rem(row_index + 1, rows_count)}, {"gy": lax.rem(row_index + rows_count - 1, rows_count)}]
    targets += [{"gx": lax.rem(col_index + 1, cols_count)}, {"gx": lax.rem(col_index + cols_count - 1, cols_count)}]
    barrier = pltpu.get_barrier_semaphore()
    for target in targets:
        pl.semaphore_signal(barrier, inc=1, device_id=target, device_id_type=pl.DeviceIdType.MESH)
    pl.semaphore_wait(barrier, len(targets))

    def spread(r, g):
        return pltpu.make_async_remote_copy(
            src_ref=spec.at[peers[r], g],
            dst_ref=got.at[me, g],
            send_sem=send1.at[r, g],
            recv_sem=recv1.at[r, g],
            device_id=targets[r],
            device_id_type=pl.DeviceIdType.MESH,
        )

    wide_lane = lax.broadcasted_iota(jnp.int32, (1, 2 * HALF), 1)
    own_mask = tissue[0].astype(F32)
    own = [coarse[0].astype(F32), coarse[1].astype(F32)]
    facts = jnp.zeros((1, 2 * HALF), F32)
    for place, fact in enumerate([own_mask] + own):
        facts = jnp.where(wide_lane == 3 * kept + place, fact, facts)

    def columns(g, carry):
        halves = []
        for q in range(2):
            packed = None
            for i in range(3):
                c = g * 3 + i
                value = rowwise[q, pl.ds(jnp.minimum(c, channels - 1), length, stride=channels), :]
                value = jnp.concatenate([value, jnp.zeros_like(value)], axis=1)
                if i == 0:
                    packed = value
                else:
                    value = value * (c < channels).astype(F32)
                    packed = packed + pltpu.roll(value, i * kept, 1)
            halves.append(packed.astype(BF))
        out = jnp.dot(left[...], jnp.concatenate(halves, axis=0), preferred_element_type=F32)
        out = (out + facts).astype(BF)
        for q in range(secs):
            spec[q, g] = out[q * size : (q + 1) * size]
        for r in range(secs - 1):
            spread(r, g).start()
        got[me, g] = spec[me, g]
        return carry

    lax.fori_loop(0, groups, columns, 0)
    acc[...] = jnp.zeros_like(acc)

    def multiply(g, carry):
        for r in range(secs - 1):
            spread(r, g).wait()
        values = [got[t, g].astype(F32) for t in range(secs)]
        for s in range(secs):
            for lag in range(1, min(s, LAGS) + 1):
                cur, ear = values[s], values[s - lag]
                acc[s, lag - 1, :half] += ear[:half] * cur[:half] + ear[half:] * cur[half:]
                acc[s, lag - 1, half:] += ear[:half] * cur[half:] - ear[half:] * cur[:half]
        return carry

    lax.fori_loop(0, groups, multiply, 0)
    for s in range(secs):
        for lag in range(LAGS):
            whole = acc[s, lag]
            total = whole[:, :HALF]
            for i in range(1, 3):
                total = total + pltpu.roll(whole, 2 * HALF - i * kept, 1)[:, :HALF]
            owed[s, lag] = total
    returns = [
        pltpu.make_async_remote_copy(
            src_ref=owed.at[peers[r]],
            dst_ref=power.at[me],
            send_sem=send2.at[r],
            recv_sem=recv2.at[r],
            device_id=targets[r],
            device_id_type=pl.DeviceIdType.MESH,
        )
        for r in range(secs - 1)
    ]
    for copy in returns:
        copy.start()
    power[me] = owed[me]

    row = lax.broadcasted_iota(jnp.int32, (length, 1), 0)
    col = lax.broadcasted_iota(jnp.int32, (1, length), 1)
    sign_y = jnp.where(row < length // 2, row, row - length).astype(F32)
    sign_x = jnp.where(col < length // 2, col, col - length).astype(F32)
    place = lax.broadcasted_iota(jnp.int32, flow.shape, 0)
    side = lax.broadcasted_iota(jnp.int32, flow.shape, 1)
    lane = lax.broadcasted_iota(jnp.int32, (1, HALF), 1)

    def pick(values, at):
        return jnp.sum(jnp.where(lane == at, values, 0.0))

    scale = 1.0 / (float(length) ** 3 * channels)
    for copy in returns:
        copy.wait()
    stacked = jnp.concatenate(
        [jnp.concatenate([power[q, lag] for q in range(secs)], axis=0) for lag in range(LAGS)], axis=1
    )
    mixed = jnp.dot(back[...], stacked, precision=lax.Precision.HIGHEST, preferred_element_type=F32)
    result = jnp.zeros(flow.shape, F32)
    pulled = [jnp.float32(0.0), jnp.float32(0.0)]
    weights, goals = [], []
    at = 3 * kept - HALF
    for lag in range(LAGS):
        part = mixed[:, lag * HALF : (lag + 1) * HALF]
        lhs = jnp.concatenate([part[:length], part[length:]], axis=1)
        scores = jnp.dot(lhs, last[...], precision=lax.Precision.HIGHEST, preferred_element_type=F32) * scale
        chances = jnp.exp(scores - jnp.max(scores))
        total = jnp.sum(chances)
        usable = (me > lag).astype(F32)
        peak = [
            usable * (jnp.sum(chances * sign_y) / total),
            usable * (jnp.sum(chances * sign_x) / total),
        ]
        prior = got[lax.rem(me + secs - lag - 1, secs), 0, 0:16, HALF : 2 * HALF].astype(F32)[0:1]
        weight = usable * LAG_WEIGHTS[lag] * own_mask * pick(prior, at)
        goal = []
        for d in range(2):
            result = jnp.where((place == lag) & (side == d), peak[d], result)
            before = pick(prior, at + 1 + d)
            goal.append(peak[d] + own[d] - before)
            pulled[d] = pulled[d] + weight * (before + goal[d] - own[d])
        weights.append(weight)
        goals.append(goal)
    flow[...] = result
    current = jnp.zeros(node.shape, F32)
    for d in range(2):
        current = jnp.where(side == d, own[d] + STEP_SIZE * pulled[d], current)
    node[...] = current
    passes = [
        pltpu.make_async_remote_copy(
            src_ref=node,
            dst_ref=beside.at[k],
            send_sem=send3.at[k],
            recv_sem=recv3.at[k],
            device_id=target,
            device_id_type=pl.DeviceIdType.MESH,
        )
        for k, target in enumerate(targets)
    ]
    for copy in passes:
        copy.start()
    for copy in passes:
        copy.wait()
    pull = jnp.zeros(node.shape, F32)
    for lag in range(LAGS):
        goal = jnp.where(side == 0, goals[lag][0], goals[lag][1])
        pull = pull + weights[lag] * (beside[lag] + goal - current)
    inside = [row_index > 0, row_index < rows_count - 1, col_index > 0, col_index < cols_count - 1]
    plane = jnp.zeros(node.shape, F32)
    for k, here in enumerate(inside):
        plane = plane + here.astype(F32) * (beside[secs - 1 + k] - current)
    nodes_out[...] = current + STEP_SIZE * (pull + PLANE_STIFF * plane)


def body(sections, first_kernel, first_bias, second_kernel, second_bias, coarse, tissue):
    length = sections.shape[-1]
    channels = first_kernel.shape[0]
    secs = lax.axis_size("sec")
    first, left, back, last = make_tables(length, secs)
    wide = length + SPAN
    image = extended(sections, (("gy", 1), ("gx", 2)), 2)[0]
    pad = wide + SPAN + 2 - image.shape[0]
    image = jnp.pad(image, ((0, pad), (0, pad)))
    across = jnp.stack([image[: wide + SPAN, b : b + wide] for b in range(3)])
    turned = image.T
    down = jnp.stack([turned[: wide + SPAN, a : a + wide] for a in range(3)])
    vmem = pl.BlockSpec(memory_space=pltpu.VMEM)
    smem = pl.BlockSpec(memory_space=pltpu.SMEM)
    lanes, cols = SPAN * channels, SPAN // 2 * channels
    depth = 12 * channels
    features, rowwise = pl.pallas_call(
        encode_kernel,
        out_shape=(
            jax.ShapeDtypeStruct((length, length * channels), BF),
            jax.ShapeDtypeStruct((2, length * channels, HALF), F32),
        ),
        in_specs=[vmem] * 7,
        out_specs=(vmem, vmem),
        scratch_shapes=[
            pltpu.VMEM((3, length, wide * channels), BF),
            pltpu.VMEM((3, wide * channels, length), BF),
            pltpu.VMEM((6 * SPAN, lanes), BF),
            pltpu.VMEM((lanes, 6 * SPAN), BF),
            pltpu.VMEM((3, depth, cols), BF),
            pltpu.VMEM((3, cols, depth), BF),
            pltpu.VMEM((8, lanes), F32),
            pltpu.VMEM((lanes, 128), F32),
            pltpu.VMEM((8, cols), F32),
            pltpu.VMEM((cols, 128), F32),
        ],
        compiler_params=pltpu.CompilerParams(vmem_limit_bytes=48 * 1024 * 1024),
        name="encode",
    )(
        across, down, first_kernel, second_kernel, first_bias[None, :], second_bias[None, :],
        jnp.asarray(first, BF),
    )
    size = 2 * length // secs
    groups = (channels + 2) // 3
    others = secs - 1
    dma = pltpu.SemaphoreType.DMA
    peaks, nodes = pl.pallas_call(
        functools.partial(mesh_kernel, channels),
        out_shape=(jax.ShapeDtypeStruct((8, 128), F32), jax.ShapeDtypeStruct((8, 128), F32)),
        in_specs=[smem, smem] + [vmem] * 4,
        out_specs=(vmem, vmem),
        scratch_shapes=[
            pltpu.VMEM((secs, groups, size, 2 * HALF), BF),
            pltpu.VMEM((secs, groups, size, 2 * HALF), BF),
            pltpu.VMEM((secs, LAGS, size, 2 * HALF), F32),
            pltpu.VMEM((secs, LAGS, size, HALF), F32),
            pltpu.VMEM((secs, LAGS, size, HALF), F32),
            pltpu.VMEM((8, 128), F32),
            pltpu.VMEM((others + 4, 8, 128), F32),
            dma((others, groups)),
            dma((others, groups)),
            dma((others,)),
            dma((others,)),
            dma((others + 4,)),
            dma((others + 4,)),
        ],
        compiler_params=pltpu.CompilerParams(
            vmem_limit_bytes=32 * 1024 * 1024, collective_id=0, has_side_effects=True
        ),
        name="mesh",
    )(
        tissue.reshape(1), coarse.reshape(2), rowwise, jnp.asarray(left, BF), jnp.asarray(back), jnp.asarray(last),
    )
    return (
        features.reshape(1, length, features.shape[-1]),
        peaks[:LAGS, :2].reshape(1, LAGS, 2, 1, 1),
        nodes[0, :2].reshape(1, 2, 1, 1),
    )


def solution(mesh):
    in_specs = (P("sec", "gy", "gx"), P(), P(), P(), P(), P("sec", None), P("sec", "gy", "gx"))
    out_specs = (P("sec", "gy", "gx"), P("sec", None, None, "gy", "gx"), P("sec", None, "gy", "gx"))
    return jax.shard_map(body, mesh=mesh, in_specs=in_specs, out_specs=out_specs, check_vma=False)
```

time: 142 us -> 89.7 us (0.63); the launches traced: 140 us -> 89.2 us
  starting transfers between devices: 41.3 us -> 9.72 us
  Pallas kernels: 33.5 us -> 63 us
  waiting for transfers between devices: 31.7 us -> 4.01 us
  local copies, waits for them, and re-layouts: 20.4 us -> 10.8 us
  matrix products: 7.75 us -> 0 us
  between operations: 3.91 us -> 1.43 us
    pallas_call x2 -> x1, Pallas kernels: 4.53 us -> 40.4 us  [body(): pl.pallas_call(functools.partial(mesh_kernel, channels), out_shape=(jax.S...]
    all_to_all x2 -> x0, waiting for transfers between devices: 29.7 us -> none  [the longest x1 29.7 us: body(): got = lax.all_to_all(spec, 'sec', 0, 0)]
    ppermute x10 -> x0, starting transfers between devices: 20.6 us -> none  [shifted(): return lax.ppermute(value, axis, pairs)]
    reshape x11 -> x1, local copies, waits for them, and re-layouts: 14.3 us -> 0.01 us  [body(): peaks[:LAGS, :2].reshape(1, LAGS, 2, 1, 1)]
    all_to_all x2 -> x0, starting transfers between devices: 9.43 us -> none  [the longest x1 5.13 us: body(): got = lax.all_to_all(spec, 'sec', 0, 0)]
    dot_general x4 -> x0, matrix products: 7.75 us -> none  [the longest x1 3.22 us: bands(): jnp.einsum('txl,catk->axklc', hot2, taps)]
    pallas_call x1, Pallas kernels: 29 us -> 22.5 us  [body(): pl.pallas_call(encode_kernel, out_shape=(jax.ShapeDtypeStruct((length, le...]
    unnamed x22 -> x19, local copies, waits for them, and re-layouts: 2.55 us -> 8.92 us
  transfers between devices with their start and end apart: 16 -> 4, of which waited for: 3 -> 2; matrix products, arithmetic and copies ran while one was open for 18% -> 2% of each run, Pallas kernels for 0% -> 0%
where the time goes in v1:
time: 89.7 us; the launch traced here: 89.2 us
  Pallas kernels  63 us (70%)
  local copies, waits for them, and re-layouts  10.8 us (12%)
  starting transfers between devices  9.72 us (11%)
  waiting for transfers between devices  4.01 us (4%)
  between operations  1.43 us (2%)
    pallas_call x1, Pallas kernels, body(): pl.pallas_call(functools.partial(mesh_kernel, channels), out_shape=(jax.S...  40.4 us
    pallas_call x1, Pallas kernels, body(): pl.pallas_call(encode_kernel, out_shape=(jax.ShapeDtypeStruct((length, le...  22.5 us
    unnamed x19, local copies, waits for them, and re-layouts  8.92 us
    ppermute x2, starting transfers between devices, extended(): lax.ppermute(tail, axis, [(i, (i + 1) % count) for i in range(ends)])  7.14 us
    ppermute x2, waiting for transfers between devices, extended(): lax.ppermute(head, axis, [((i + 1) % count, i) for i in range(ends)])  4.01 us
    ppermute x2, starting transfers between devices, extended(): lax.ppermute(head, axis, [((i + 1) % count, i) for i in range(ends)])  2.58 us
  transfers between devices with their start and end apart: 4, of which 2 were waited for; matrix products, arithmetic and copies ran while one was open for 2% of the time, Pallas kernels for 0%

profile of v1, /device:TPU:1, one launch (start us, length us, event | category | flops | bytes accessed | tf_op | source)
XLA Modules:
  0.0 89.2 jit_solution(2056832902537252562)
XLA Ops:
  0.6 0.7 fusion.3
  1.3 0.1 copy.14
  1.5 3.9 %collective-permute-start = (bf16[1,2,160]{1,2,0:T(8,128)(2,1)S(1)}, bf16[1,2,160]{1,2,0:T(8,128)(2,1)S(1)}, u32[]{:S(2)}, u32[]{:S(2)}) collective-permute-start(bf16[1,2,160]{1,2,0:T(8,128)(2,1)S(1)} %copy.14), channel_id=1, source_target_pairs={{0,4},{1,5},{2,6},{3,7},{8,12},{9,13},{10,14},{11,15},{16,20},{17,... | collective-permute-start | bytes 1928 | tf_op jit(solution)/shard_map/ppermute | solution.py:30
  5.4 0.1 copy.15
  5.6 1.3 %collective-permute-start.1 = (bf16[1,2,160]{1,2,0:T(8,128)(2,1)S(1)}, bf16[1,2,160]{1,2,0:T(8,128)(2,1)S(1)}, u32[]{:S(2)}, u32[]{:S(2)}) collective-permute-start(bf16[1,2,160]{1,2,0:T(8,128)(2,1)S(1)} %copy.15), channel_id=1, source_target_pairs={{4,0},{5,1},{6,2},{7,3},{12,8},{13,9},{14,10},{15,11},{20,16},{21,... | collective-permute-start | bytes 1928 | tf_op jit(solution)/shard_map/ppermute | solution.py:32
  6.9 1.0 %copy.16 = bf16[1,160,160]{1,2,0:T(8,128)(2,1)S(1)} copy(bf16[1,160,160]{2,1,0:T(8,128)(2,1)} %param.11) | data formatting | bytes 102400 | tf_op args[0]
  7.9 0.0 collective-permute-done
  7.9 2.4 %collective-permute-done.1 = bf16[1,2,160]{1,2,0:T(8,128)(2,1)S(1)} collective-permute-done((bf16[1,2,160]{1,2,0:T(8,128)(2,1)S(1)}, bf16[1,2,160]{1,2,0:T(8,128)(2,1)S(1)}, u32[]{:S(2)}, u32[]{:S(2)}) %collective-permute-start.1) | collective-permute-done | bytes 672 | tf_op jit(solution)/shard_map/ppermute | solution.py:32
  10.3 0.1 pad_maximum_fusion.4
  10.4 3.2 %collective-permute-start.2 = (bf16[1,164,2]{1,2,0:T(2,128)(2,1)S(1)}, bf16[1,164,2]{1,2,0:T(2,128)(2,1)S(1)}, u32[]{:S(2)}, u32[]{:S(2)}) collective-permute-start(bf16[1,164,2]{1,2,0:T(2,128)(2,1)S(1)} %get-tuple-element.14), channel_id=1, source_target_pairs={{0,1},{1,2},{2,3},{4,5},{5,6},{6,7},{8,9},{9,10},{10,11},{12,13},{... | collective-permute-start | bytes 1976 | tf_op jit(solution)/shard_map/ppermute | solution.py:30
  13.6 1.3 %collective-permute-start.3 = (bf16[1,164,2]{1,2,0:T(2,128)(2,1)S(1)}, bf16[1,164,2]{1,2,0:T(2,128)(2,1)S(1)}, u32[]{:S(2)}, u32[]{:S(2)}) collective-permute-start(bf16[1,164,2]{1,2,0:T(2,128)(2,1)S(1)} %get-tuple-element.15), channel_id=1, source_target_pairs={{1,0},{2,1},{3,2},{5,4},{6,5},{7,6},{9,8},{10,9},{11,10},{13,12},{... | collective-permute-start | bytes 1976 | tf_op jit(solution)/shard_map/ppermute | solution.py:32
  14.9 0.8 copy.18.kernel1
  16.3 0.0 collective-permute-done.2
  16.3 1.6 %collective-permute-done.3 = bf16[1,164,2]{1,2,0:T(2,128)(2,1)S(1)} collective-permute-done((bf16[1,164,2]{1,2,0:T(2,128)(2,1)S(1)}, bf16[1,164,2]{1,2,0:T(2,128)(2,1)S(1)}, u32[]{:S(2)}, u32[]{:S(2)}) %collective-permute-start.3) | collective-permute-done | bytes 688 | tf_op jit(solution)/shard_map/ppermute | solution.py:32
  17.9 0.1 maximum_bitcast_fusion
  18.1 0.1 slice_bitcast_fusion.2
  18.2 0.1 pad_maximum_fusion.1
  18.3 0.2 copy.17.across
  18.5 0.1 pad_maximum_fusion.down
  18.6 0.0 copy-start.3
  18.6 0.9 copy-done.3
  19.4 0.7 copy-done.4
  20.2 0.7 copy-done.5
  20.8 0.7 copy-done.6
  21.5 22.5 %encode.1 = (bf16[160,5120]{1,0:T(8,128)(2,1)}, f32[2,5120,128]{2,1,0:T(8,128)S(1)}) custom-call(bf16[3,192,176]{2,1,0:T(8,128)(2,1)S(1)} %copy.17.across, bf16[3,192,176]{2,1,0:T(8,128)(2,1)S(1)} %pad_maximum_fusion.down, bf16[32,9]{1,0:T(8,128)(2,1)S(1)} %copy.18.kernel1, bf16[32,288]{1,0:T(8,128)(2,1)S(1)} %copy-done.4, bf16[1,32]{1,0:T(2,128)(2,1)S(1)} %bitcast.26, ...), custom_call_target="tpu_custom_call" | custom-call | tf_op jit(solution)/shard_map/encode/pallas_call | solution.py:371
  44.0 1.0 %copy-done = f32[320,320]{1,0:T(8,128)S(1)} copy-done((f32[320,320]{1,0:T(8,128)S(1)}, f32[320,320]{1,0:T(8,128)}, u32[]{:S(2)}) %copy-start) | copy-done | bytes 409624
  45.1 0.9 %copy-done.1 = f32[256,160]{1,0:T(8,128)S(1)} copy-done((f32[256,160]{1,0:T(8,128)S(1)}, f32[256,160]{1,0:T(8,128)}, u32[]{:S(2)}) %copy-start.1) | copy-done | bytes 163864
  46.0 0.9 %copy-done.2 = bf16[320,320]{1,0:T(8,128)(2,1)S(1)} copy-done((bf16[320,320]{1,0:T(8,128)(2,1)S(1)}, bf16[320,320]{1,0:T(8,128)(2,1)}, u32[]{:S(2)}) %copy-start.2) | copy-done | bytes 204824
  47.0 0.7 copy-done.7
  47.6 40.4 %mesh.1 = (f32[8,128]{1,0:T(8,128)S(1)}, f32[8,128]{1,0:T(8,128)S(1)}) custom-call(s32[1]{0:T(128)} %bitcast.25.tissue, s32[2]{0:T(128)S(1)} %bitcast.28, f32[2,5120,128]{2,1,0:T(8,128)S(1)} %get-tuple-element.8.rowwise, bf16[320,320]{1,0:T(8,128)(2,1)S(1)} %copy-done.2, f32[320,320]{1,0:T(8,128)S(1)} %copy-done, f32[256,160]{1,0:T(8,128)S(1)} %copy-done.1), custom_call_target="tpu_custom_call" | custom-call | tf_op jit(solution)/shard_map/mesh/pallas_call | solution.py:401
  88.0 0.6 copy.20
  88.7 0.5 slice_bitcast_fusion.4
  (10 shorter events, 0.1 us)
Async XLA Ops:
  1.5 6.4 %collective-permute-start = (bf16[1,2,160]{1,2,0:T(8,128)(2,1)S(1)}, bf16[1,2,160]{1,2,0:T(8,128)(2,1)S(1)}, u32[]{:S(2)}, u32[]{:S(2)}) collective-permute-start(bf16[1,2,160]{1,2,0:T(8,128)(2,1)S(1)} %copy.14), channel_id=1, source_target_pairs={{0,4},{1,5},{2,6},{3,7},{8,12},{9,13},{10,14},{11,15},{16,20},{17,... | collective-permute-start | bytes 1928 | tf_op jit(solution)/shard_map/ppermute | solution.py:30
  5.6 4.7 %collective-permute-start.1 = (bf16[1,2,160]{1,2,0:T(8,128)(2,1)S(1)}, bf16[1,2,160]{1,2,0:T(8,128)(2,1)S(1)}, u32[]{:S(2)}, u32[]{:S(2)}) collective-permute-start(bf16[1,2,160]{1,2,0:T(8,128)(2,1)S(1)} %copy.15), channel_id=1, source_target_pairs={{4,0},{5,1},{6,2},{7,3},{12,8},{13,9},{14,10},{15,11},{20,16},{21,... | collective-permute-start | bytes 1928 | tf_op jit(solution)/shard_map/ppermute | solution.py:32
  10.4 5.9 %collective-permute-start.2 = (bf16[1,164,2]{1,2,0:T(2,128)(2,1)S(1)}, bf16[1,164,2]{1,2,0:T(2,128)(2,1)S(1)}, u32[]{:S(2)}, u32[]{:S(2)}) collective-permute-start(bf16[1,164,2]{1,2,0:T(2,128)(2,1)S(1)} %get-tuple-element.14), channel_id=1, source_target_pairs={{0,1},{1,2},{2,3},{4,5},{5,6},{6,7},{8,9},{9,10},{10,11},{12,13},{... | collective-permute-start | bytes 1976 | tf_op jit(solution)/shard_map/ppermute | solution.py:30
  13.6 4.3 %collective-permute-start.3 = (bf16[1,164,2]{1,2,0:T(2,128)(2,1)S(1)}, bf16[1,164,2]{1,2,0:T(2,128)(2,1)S(1)}, u32[]{:S(2)}, u32[]{:S(2)}) collective-permute-start(bf16[1,164,2]{1,2,0:T(2,128)(2,1)S(1)} %get-tuple-element.15), channel_id=1, source_target_pairs={{1,0},{2,1},{3,2},{5,4},{6,5},{7,6},{9,8},{10,9},{11,10},{13,12},{... | collective-permute-start | bytes 1976 | tf_op jit(solution)/shard_map/ppermute | solution.py:32
  18.6 0.9 copy-start.3
  19.4 0.7 copy-start.4
  20.2 0.7 copy-start.5
  20.8 0.7 copy-start.6
  44.0 1.0 %copy-start = (f32[320,320]{1,0:T(8,128)S(1)}, f32[320,320]{1,0:T(8,128)}, u32[]{:S(2)}) copy-start(f32[320,320]{1,0:T(8,128)} %constant.13.clone.back) | copy-start | bytes 1228804
  45.1 0.9 %copy-start.1 = (f32[256,160]{1,0:T(8,128)S(1)}, f32[256,160]{1,0:T(8,128)}, u32[]{:S(2)}) copy-start(f32[256,160]{1,0:T(8,128)} %constant.14.clone.last) | copy-start | bytes 491524
  46.0 0.9 %copy-start.2 = (bf16[320,320]{1,0:T(8,128)(2,1)S(1)}, bf16[320,320]{1,0:T(8,128)(2,1)}, u32[]{:S(2)}) copy-start(bf16[320,320]{1,0:T(8,128)(2,1)} %constant.12.clone.left) | copy-start | bytes 614404
  47.0 0.7 copy-start.7

commit v2 on v1

--- a/solution.py
+++ b/solution.py
@@ -19,21 +19,73 @@
 F32 = jnp.float32
 
 
-def extended(cells, sides, width):
-    for axis, dim in sides:
-        count = lax.axis_size(axis)
-        ends = count - 1
-        head = lax.slice_in_dim(cells, 0, width, axis=dim)
-        tail = lax.slice_in_dim(cells, cells.shape[dim] - width, cells.shape[dim], axis=dim)
-        cells = jnp.concatenate(
-            [
-                lax.ppermute(tail, axis, [(i, (i + 1) % count) for i in range(ends)]),
-                cells,
-                lax.ppermute(head, axis, [((i + 1) % count, i) for i in range(ends)]),
-            ],
-            axis=dim,
+def halo_kernel(image, across, down, strips, landed, ext, send, recv):
+    length = image.shape[0]
+    tall, wide = across.shape[1], across.shape[2]
+    row_index, rows_count = lax.axis_index("gy"), lax.axis_size("gy")
+    col_index, cols_count = lax.axis_index("gx"), lax.axis_size("gx")
+    routes = [(dy, dx, 0 if dy < 0 else 1) for dy in (-1, 1) for dx in (-1, 0, 1)] + [(0, -1, 2), (0, 1, 3)]
+    targets = [
+        {
+            "gy": lax.rem(row_index + dy + rows_count, rows_count),
+            "gx": lax.rem(col_index + dx + cols_count, cols_count),
+        }
+        for dy, dx, _ in routes
+    ]
+    barrier = pltpu.get_barrier_semaphore()
+    for target in targets:
+        pl.semaphore_signal(barrier, inc=1, device_id=target, device_id_type=pl.DeviceIdType.MESH)
+    own = image[...].astype(F32)
+    turned = jnp.transpose(own)
+    strips[0] = image[:SPAN]
+    strips[1] = image[length - SPAN :]
+    strips[2] = turned[:SPAN].astype(BF)
+    strips[3] = turned[length - SPAN :].astype(BF)
+    pl.semaphore_wait(barrier, len(targets))
+    copies = [
+        pltpu.make_async_remote_copy(
+            src_ref=strips.at[strip],
+            dst_ref=landed.at[k],
+            send_sem=send.at[k],
+            recv_sem=recv.at[k],
+            device_id=targets[k],
+            device_id_type=pl.DeviceIdType.MESH,
         )
-    return cells
+        for k, (_, _, strip) in enumerate(routes)
+    ]
+    for copy in copies:
+        copy.start()
+    ext[...] = jnp.zeros_like(ext)
+    ext[2 : length + 2, 2 : length + 2] = own
+    for copy in copies:
+        copy.wait()
+    end = length + 2
+    for k, (dy, dx, _) in enumerate(routes):
+        here = jnp.logical_and(
+            jnp.logical_and(row_index - dy >= 0, row_index - dy < rows_count),
+            jnp.logical_and(col_index - dx >= 0, col_index - dx < cols_count),
+        ).astype(F32)
+        strip = landed[k].astype(F32) * here
+        if dy == 0:
+            strip = jnp.transpose(strip)
+            if dx > 0:
+                ext[2:end, 0:2] = strip[:, SPAN - 2 :]
+            else:
+                ext[2:end, end : end + 2] = strip[:, :2]
+            continue
+        part = strip[SPAN - 2 :] if dy > 0 else strip[:2]
+        r0 = 0 if dy > 0 else end
+        if dx == 0:
+            ext[r0 : r0 + 2, 2:end] = part
+        elif dx > 0:
+            ext[r0 : r0 + 2, 0:2] = part[:, length - 2 :]
+        else:
+            ext[r0 : r0 + 2, end : end + 2] = part[:, :2]
+    whole = ext[...]
+    turned = jnp.transpose(whole)
+    for k in range(3):
+        across[k] = whole[:tall, k : k + wide].astype(BF)
+        down[k] = turned[:tall, k : k + wide].astype(BF)
 
 
 def make_tables(length, parts):
@@ -176,14 +228,20 @@
         rowwise[1, pl.ds(c0, cols), :] = pair[:, HALF:]
         return carry
 
-    lax.fori_loop(0, length * channels // cols, second_layer, 0)
+    lax.fori_loop(0, length * channels // cols, second_layer, 0, unroll=4)
 
 
 def mesh_kernel(
-    channels, tissue, coarse, rowwise, left, back, last, flow, nodes_out,
-    spec, got, acc, owed, power, node, beside,
-    send1, recv1, send2, recv2, send3, recv3,
+    channels, tissue, coarse, rowwise, left, back_far, last_far, flow, nodes_out,
+    back, last, spec, got, acc, owed, power, node, beside,
+    send1, recv1, send2, recv2, send3, recv3, fetched,
 ):
+    fetches = [
+        pltpu.make_async_copy(back_far, back, fetched.at[0]),
+        pltpu.make_async_copy(last_far, last, fetched.at[1]),
+    ]
+    for fetch in fetches:
+        fetch.start()
     me = lax.axis_index("sec")
     secs = lax.axis_size("sec")
     row_index, rows_count = lax.axis_index("gy"), lax.axis_size("gy")
@@ -292,6 +350,8 @@
     scale = 1.0 / (float(length) ** 3 * channels)
     for copy in returns:
         copy.wait()
+    for fetch in fetches:
+        fetch.wait()
     stacked = jnp.concatenate(
         [jnp.concatenate([power[q, lag] for q in range(secs)], axis=0) for lag in range(LAGS)], axis=1
     )
@@ -358,13 +418,27 @@
     secs = lax.axis_size("sec")
     first, left, back, last = make_tables(length, secs)
     wide = length + SPAN
-    image = extended(sections, (("gy", 1), ("gx", 2)), 2)[0]
-    pad = wide + SPAN + 2 - image.shape[0]
-    image = jnp.pad(image, ((0, pad), (0, pad)))
-    across = jnp.stack([image[: wide + SPAN, b : b + wide] for b in range(3)])
-    turned = image.T
-    down = jnp.stack([turned[: wide + SPAN, a : a + wide] for a in range(3)])
     vmem = pl.BlockSpec(memory_space=pltpu.VMEM)
+    dma = pltpu.SemaphoreType.DMA
+    tall = wide + SPAN
+    frame = jax.ShapeDtypeStruct((3, tall, wide), BF)
+    across, down = pl.pallas_call(
+        halo_kernel,
+        out_shape=(frame, frame),
+        in_specs=[vmem],
+        out_specs=(vmem, vmem),
+        scratch_shapes=[
+            pltpu.VMEM((4, SPAN, length), BF),
+            pltpu.VMEM((8, SPAN, length), BF),
+            pltpu.VMEM((256, 256), F32),
+            dma((8,)),
+            dma((8,)),
+        ],
+        compiler_params=pltpu.CompilerParams(
+            vmem_limit_bytes=16 * 1024 * 1024, collective_id=1, has_side_effects=True
+        ),
+        name="halo",
+    )(sections[0])
     smem = pl.BlockSpec(memory_space=pltpu.SMEM)
     lanes, cols = SPAN * channels, SPAN // 2 * channels
     depth = 12 * channels
@@ -397,13 +471,14 @@
     size = 2 * length // secs
     groups = (channels + 2) // 3
     others = secs - 1
-    dma = pltpu.SemaphoreType.DMA
     peaks, nodes = pl.pallas_call(
         functools.partial(mesh_kernel, channels),
         out_shape=(jax.ShapeDtypeStruct((8, 128), F32), jax.ShapeDtypeStruct((8, 128), F32)),
-        in_specs=[smem, smem] + [vmem] * 4,
+        in_specs=[smem, smem] + [vmem] * 2 + [pl.BlockSpec(memory_space=pltpu.HBM)] * 2,
         out_specs=(vmem, vmem),
         scratch_shapes=[
+            pltpu.VMEM(back.shape, F32),
+            pltpu.VMEM(last.shape, F32),
             pltpu.VMEM((secs, groups, size, 2 * HALF), BF),
             pltpu.VMEM((secs, groups, size, 2 * HALF), BF),
             pltpu.VMEM((secs, LAGS, size, 2 * HALF), F32),
@@ -417,6 +492,7 @@
             dma((others,)),
             dma((others + 4,)),
             dma((others + 4,)),
+            dma((2,)),
         ],
         compiler_params=pltpu.CompilerParams(
             vmem_limit_bytes=32 * 1024 * 1024, collective_id=0, has_side_effects=True

time: 89.7 us -> 80.9 us (0.902)
  starting transfers between devices: 9.72 us -> 0 us
  Pallas kernels: 63 us -> 69.8 us
  waiting for transfers between devices: 4.01 us -> 0 us
  local copies, waits for them, and re-layouts: 10.8 us -> 9.33 us
    ppermute x4 -> x0, starting transfers between devices: 9.72 us -> none  [the longest x2 7.14 us: extended(): lax.ppermute(tail, axis, [(i, (i + 1) % count) for i in range(ends)])]
    pallas_call x0 -> x1, Pallas kernels: none -> 7.53 us  [body(): pl.pallas_call(halo_kernel, out_shape=(frame, frame), in_specs=[vmem], ou...]
    ppermute x4 -> x0, waiting for transfers between devices: 4.01 us -> none  [the longest x2 4.01 us: extended(): lax.ppermute(head, axis, [((i + 1) % count, i) for i in range(ends)])]
    slice x3 -> x0, local copies, waits for them, and re-layouts: 0.98 us -> none  [the longest x2 0.85 us: extended(): lax.slice_in_dim(cells, cells.shape[dim] - width, cells.shape[dim], axis=...]
    unnamed x19 -> x20, local copies, waits for them, and re-layouts: 8.92 us -> 8.82 us
  transfers between devices with their start and end apart: 4 -> 0, of which waited for: 2 -> 0; matrix products, arithmetic and copies ran while one was open for 2% -> 0% of each run, Pallas kernels for 0% -> 0%
where the time goes in v2:
time: 80.9 us; the launch traced here: 80.5 us
  Pallas kernels  69.8 us (86%)
  local copies, waits for them, and re-layouts  9.33 us (12%)
  between operations  1.33 us (2%)
    pallas_call x1, Pallas kernels, body(): pl.pallas_call(functools.partial(mesh_kernel, channels), out_shape=(jax.S...  40.2 us
    pallas_call x1, Pallas kernels, body(): pl.pallas_call(encode_kernel, out_shape=(jax.ShapeDtypeStruct((length, le...  22.1 us
    unnamed x20, local copies, waits for them, and re-layouts  8.82 us
    pallas_call x1, Pallas kernels, body(): pl.pallas_call(halo_kernel, out_shape=(frame, frame), in_specs=[vmem], ou...  7.53 us

profile of v2, /device:TPU:1, one launch (start us, length us, event | category | flops | bytes accessed | tf_op | source)
XLA Modules:
  0.0 80.5 jit_solution(155902818436442769)
XLA Ops:
  0.6 0.0 copy-start.3
  0.6 0.9 %copy-done.3 = bf16[1,160,160]{2,1,0:T(8,128)(2,1)S(1)} copy-done((bf16[1,160,160]{2,1,0:T(8,128)(2,1)S(1)}, bf16[1,160,160]{2,1,0:T(8,128)(2,1)}, u32[]{:S(2)}) %copy-start.3) | copy-done | bytes 51224
  1.5 7.5 %halo.1 = (bf16[3,192,176]{2,1,0:T(8,128)(2,1)S(1)}, bf16[3,192,176]{2,1,0:T(8,128)(2,1)S(1)}) custom-call(bf16[160,160]{1,0:T(8,128)(2,1)S(1)} %bitcast.11), custom_call_target="tpu_custom_call" | custom-call | tf_op jit(solution)/shard_map/halo/pallas_call | solution.py:425
  9.1 0.8 copy.14.kernel1
  9.8 0.0 copy-start.4
  9.8 0.9 %copy-done.4 = bf16[160,256]{1,0:T(8,128)(2,1)S(1)} copy-done((bf16[160,256]{1,0:T(8,128)(2,1)S(1)}, bf16[160,256]{1,0:T(8,128)(2,1)}, u32[]{:S(2)}) %copy-start.4) | copy-done | bytes 81944
  10.7 0.0 copy-start.5
  10.7 0.7 copy-done.5
  11.5 0.0 copy-start.6
  11.5 0.7 copy-done.6
  12.1 0.0 copy-start.7
  12.1 0.7 copy-done.7
  12.8 22.1 %encode.1 = (bf16[160,5120]{1,0:T(8,128)(2,1)}, f32[2,5120,128]{2,1,0:T(8,128)S(1)}) custom-call(bf16[3,192,176]{2,1,0:T(8,128)(2,1)S(1)} %get-tuple-element.9.across, bf16[3,192,176]{2,1,0:T(8,128)(2,1)S(1)} %get-tuple-element.10.down, bf16[32,9]{1,0:T(8,128)(2,1)S(1)} %copy.14.kernel1, bf16[32,288]{1,0:T(8,128)(2,1)S(1)} %copy-done.5, ...), custom_call_target="tpu_custom_call" | custom-call | tf_op jit(solution)/shard_map/encode/pallas_call | solution.py:445
  35.5 0.0 copy-start
  35.5 1.0 %copy-done = f32[320,320]{1,0:T(8,128)S(1)} copy-done((f32[320,320]{1,0:T(8,128)S(1)}, f32[320,320]{1,0:T(8,128)}, u32[]{:S(2)}) %copy-start) | copy-done | bytes 409624
  36.5 0.0 copy-start.1
  36.5 0.9 %copy-done.1 = f32[256,160]{1,0:T(8,128)S(1)} copy-done((f32[256,160]{1,0:T(8,128)S(1)}, f32[256,160]{1,0:T(8,128)}, u32[]{:S(2)}) %copy-start.1) | copy-done | bytes 163864
  37.5 0.0 copy-start.2
  37.5 0.9 %copy-done.2 = bf16[320,320]{1,0:T(8,128)(2,1)S(1)} copy-done((bf16[320,320]{1,0:T(8,128)(2,1)S(1)}, bf16[320,320]{1,0:T(8,128)(2,1)}, u32[]{:S(2)}) %copy-start.2) | copy-done | bytes 204824
  38.4 0.0 copy-start.8
  38.4 0.7 copy-done.8
  39.1 40.2 %mesh.1 = (f32[8,128]{1,0:T(8,128)S(1)}, f32[8,128]{1,0:T(8,128)S(1)}) custom-call(s32[1]{0:T(128)} %bitcast.10.tissue, s32[2]{0:T(128)S(1)} %bitcast.14, f32[2,5120,128]{2,1,0:T(8,128)S(1)} %get-tuple-element.12.rowwise, bf16[320,320]{1,0:T(8,128)(2,1)S(1)} %copy-done.2, f32[320,320]{1,0:T(8,128)S(1)} %copy-done, f32[256,160]{1,0:T(8,128)S(1)} %copy-done.1), custom_call_target="tpu_custom_call" | custom-call | tf_op jit(solution)/shard_map/mesh/pallas_call | solution.py:474
  79.3 0.6 copy.16
  80.0 0.5 slice_bitcast_fusion.1
  (1 shorter events, 0.0 us)
Async XLA Ops:
  0.6 0.9 %copy-start.3 = (bf16[1,160,160]{2,1,0:T(8,128)(2,1)S(1)}, bf16[1,160,160]{2,1,0:T(8,128)(2,1)}, u32[]{:S(2)}) copy-start(bf16[1,160,160]{2,1,0:T(8,128)(2,1)} %param.11) | copy-start | bytes 153604
  9.8 0.9 %copy-start.4 = (bf16[160,256]{1,0:T(8,128)(2,1)S(1)}, bf16[160,256]{1,0:T(8,128)(2,1)}, u32[]{:S(2)}) copy-start(bf16[160,256]{1,0:T(8,128)(2,1)} %constant.8.clone.first) | copy-start | bytes 245764
  10.7 0.7 copy-start.5
  11.5 0.7 copy-start.6
  12.1 0.7 copy-start.7
  35.5 1.0 %copy-start = (f32[320,320]{1,0:T(8,128)S(1)}, f32[320,320]{1,0:T(8,128)}, u32[]{:S(2)}) copy-start(f32[320,320]{1,0:T(8,128)} %constant.10.clone.back_far) | copy-start | bytes 1228804
  36.5 0.9 %copy-start.1 = (f32[256,160]{1,0:T(8,128)S(1)}, f32[256,160]{1,0:T(8,128)}, u32[]{:S(2)}) copy-start(f32[256,160]{1,0:T(8,128)} %constant.11.clone.last_far) | copy-start | bytes 491524
  37.5 0.9 %copy-start.2 = (bf16[320,320]{1,0:T(8,128)(2,1)S(1)}, bf16[320,320]{1,0:T(8,128)(2,1)}, u32[]{:S(2)}) copy-start(bf16[320,320]{1,0:T(8,128)(2,1)} %constant.9.clone.left) | copy-start | bytes 614404
  38.4 0.7 copy-start.8

commit v3 on v2

--- a/solution.py
+++ b/solution.py
@@ -216,13 +216,12 @@
 
     def second_layer(blk, carry):
         c0 = pl.multiple_of(blk * cols, cols)
-        acc = bias2[0:1] + jnp.dot(hid[0, :, pl.ds(c0, depth)], band2[0], preferred_element_type=F32)
-        for a in range(1, 3):
-            acc = acc + jnp.dot(hid[a, :, pl.ds(c0, depth)], band2[a], preferred_element_type=F32)
+        window = jnp.concatenate([hid[a, :, pl.ds(c0, depth)] for a in range(3)], axis=1)
+        acc = bias2[0:1] + jnp.dot(window, band2[...].reshape(3 * depth, cols), preferred_element_type=F32)
         feat[:, pl.ds(c0, cols)] = acc.astype(BF)
-        acc = bias2t[:, 0:1] + jnp.dot(band2t[0], hidt[0, pl.ds(c0, depth), :], preferred_element_type=F32)
-        for b in range(1, 3):
-            acc = acc + jnp.dot(band2t[b], hidt[b, pl.ds(c0, depth), :], preferred_element_type=F32)
+        window = jnp.concatenate([hidt[b, pl.ds(c0, depth), :] for b in range(3)], axis=0)
+        band = jnp.concatenate([band2t[b] for b in range(3)], axis=1)
+        acc = bias2t[:, 0:1] + jnp.dot(band, window, preferred_element_type=F32)
         pair = jnp.dot(acc.astype(BF), first[...], preferred_element_type=F32)
         rowwise[0, pl.ds(c0, cols), :] = pair[:, :HALF]
         rowwise[1, pl.ds(c0, cols), :] = pair[:, HALF:]
@@ -232,22 +231,18 @@
 
 
 def mesh_kernel(
-    channels, tissue, coarse, rowwise, left, back_far, last_far, flow, nodes_out,
-    back, last, spec, got, acc, owed, power, node, beside,
-    send1, recv1, send2, recv2, send3, recv3, fetched,
+    channels, tissue, coarse, rowwise, tables, flow, nodes_out,
+    left, spec, got, acc, owed, power, node, beside,
+    send1, recv1, send2, recv2, send3, recv3,
 ):
-    fetches = [
-        pltpu.make_async_copy(back_far, back, fetched.at[0]),
-        pltpu.make_async_copy(last_far, last, fetched.at[1]),
-    ]
-    for fetch in fetches:
-        fetch.start()
     me = lax.axis_index("sec")
     secs = lax.axis_size("sec")
     row_index, rows_count = lax.axis_index("gy"), lax.axis_size("gy")
     col_index, cols_count = lax.axis_index("gx"), lax.axis_size("gx")
-    length = last.shape[1]
+    length = rowwise.shape[1] // channels
     kept = length // 2 + 1
+    double = 2 * length
+    apart = -(-double // HALF) * HALF
     groups, size = spec.shape[1], spec.shape[2]
     half = size // 2
     peers = [lax.rem(me + r, secs) for r in range(1, secs)]
@@ -257,6 +252,7 @@
     barrier = pltpu.get_barrier_semaphore()
     for target in targets:
         pl.semaphore_signal(barrier, inc=1, device_id=target, device_id_type=pl.DeviceIdType.MESH)
+    left[...] = tables[:, :double].astype(BF)
     pl.semaphore_wait(barrier, len(targets))
 
     def spread(r, g):
@@ -350,12 +346,11 @@
     scale = 1.0 / (float(length) ** 3 * channels)
     for copy in returns:
         copy.wait()
-    for fetch in fetches:
-        fetch.wait()
+    last = tables[: 2 * HALF, 2 * apart : 2 * apart + length]
     stacked = jnp.concatenate(
         [jnp.concatenate([power[q, lag] for q in range(secs)], axis=0) for lag in range(LAGS)], axis=1
     )
-    mixed = jnp.dot(back[...], stacked, precision=lax.Precision.HIGHEST, preferred_element_type=F32)
+    mixed = jnp.dot(tables[:, apart : apart + double], stacked, precision=lax.Precision.HIGHEST, preferred_element_type=F32)
     result = jnp.zeros(flow.shape, F32)
     pulled = [jnp.float32(0.0), jnp.float32(0.0)]
     weights, goals = [], []
@@ -363,7 +358,7 @@
     for lag in range(LAGS):
         part = mixed[:, lag * HALF : (lag + 1) * HALF]
         lhs = jnp.concatenate([part[:length], part[length:]], axis=1)
-        scores = jnp.dot(lhs, last[...], precision=lax.Precision.HIGHEST, preferred_element_type=F32) * scale
+        scores = jnp.dot(lhs, last, precision=lax.Precision.HIGHEST, preferred_element_type=F32) * scale
         chances = jnp.exp(scores - jnp.max(scores))
         total = jnp.sum(chances)
         usable = (me > lag).astype(F32)
@@ -435,7 +430,7 @@
             dma((8,)),
         ],
         compiler_params=pltpu.CompilerParams(
-            vmem_limit_bytes=16 * 1024 * 1024, collective_id=1, has_side_effects=True
+            vmem_limit_bytes=8 * 1024 * 1024, collective_id=1, has_side_effects=True
         ),
         name="halo",
     )(sections[0])
@@ -462,23 +457,27 @@
             pltpu.VMEM((8, cols), F32),
             pltpu.VMEM((cols, 128), F32),
         ],
-        compiler_params=pltpu.CompilerParams(vmem_limit_bytes=48 * 1024 * 1024),
+        compiler_params=pltpu.CompilerParams(vmem_limit_bytes=26 * 1024 * 1024),
         name="encode",
     )(
         across, down, first_kernel, second_kernel, first_bias[None, :], second_bias[None, :],
         jnp.asarray(first, BF),
     )
     size = 2 * length // secs
+    apart = -(-2 * length // HALF) * HALF
+    joined = np.zeros((2 * length, 2 * apart + 2 * HALF), np.float32)
+    joined[:, : 2 * length] = left
+    joined[:, apart : apart + 2 * length] = back
+    joined[: 2 * HALF, 2 * apart : 2 * apart + length] = last
     groups = (channels + 2) // 3
     others = secs - 1
     peaks, nodes = pl.pallas_call(
         functools.partial(mesh_kernel, channels),
         out_shape=(jax.ShapeDtypeStruct((8, 128), F32), jax.ShapeDtypeStruct((8, 128), F32)),
-        in_specs=[smem, smem] + [vmem] * 2 + [pl.BlockSpec(memory_space=pltpu.HBM)] * 2,
+        in_specs=[smem, smem] + [vmem] * 2,
         out_specs=(vmem, vmem),
         scratch_shapes=[
-            pltpu.VMEM(back.shape, F32),
-            pltpu.VMEM(last.shape, F32),
+            pltpu.VMEM(left.shape, BF),
             pltpu.VMEM((secs, groups, size, 2 * HALF), BF),
             pltpu.VMEM((secs, groups, size, 2 * HALF), BF),
             pltpu.VMEM((secs, LAGS, size, 2 * HALF), F32),
@@ -492,14 +491,13 @@
             dma((others,)),
             dma((others + 4,)),
             dma((others + 4,)),
-            dma((2,)),
         ],
         compiler_params=pltpu.CompilerParams(
-            vmem_limit_bytes=32 * 1024 * 1024, collective_id=0, has_side_effects=True
+            vmem_limit_bytes=18 * 1024 * 1024, collective_id=0, has_side_effects=True
         ),
         name="mesh",
     )(
-        tissue.reshape(1), coarse.reshape(2), rowwise, jnp.asarray(left, BF), jnp.asarray(back), jnp.asarray(last),
+        tissue.reshape(1), coarse.reshape(2), rowwise, jnp.asarray(joined),
     )
     return (
         features.reshape(1, length, features.shape[-1]),

time: 80.9 us -> 74 us (0.915)
  Pallas kernels: 69.8 us -> 64.6 us
  local copies, waits for them, and re-layouts: 9.33 us -> 7.72 us
    pallas_call x1, Pallas kernels: 22.1 us -> 17.2 us  [body(): pl.pallas_call(encode_kernel, out_shape=(jax.ShapeDtypeStruct((length, le...]
    unnamed x20 -> x16, local copies, waits for them, and re-layouts: 8.82 us -> 7.21 us
where the time goes in v3:
time: 74 us; the launch traced here: 73.7 us
  Pallas kernels  64.6 us (87%)
  local copies, waits for them, and re-layouts  7.72 us (10%)
  between operations  1.33 us (2%)
    pallas_call x1, Pallas kernels, body(): pl.pallas_call(functools.partial(mesh_kernel, channels), out_shape=(jax.S...  39.9 us
    pallas_call x1, Pallas kernels, body(): pl.pallas_call(encode_kernel, out_shape=(jax.ShapeDtypeStruct((length, le...  17.2 us
    pallas_call x1, Pallas kernels, body(): pl.pallas_call(halo_kernel, out_shape=(frame, frame), in_specs=[vmem], ou...  7.53 us
    unnamed x16, local copies, waits for them, and re-layouts  7.21 us

profile of v3, /device:TPU:1, one launch (start us, length us, event | category | flops | bytes accessed | tf_op | source)
XLA Modules:
  0.0 73.7 jit_solution(1742185729882946928)
XLA Ops:
  0.6 0.0 copy-start.1
  0.6 0.9 %copy-done.1 = bf16[1,160,160]{2,1,0:T(8,128)(2,1)S(1)} copy-done((bf16[1,160,160]{2,1,0:T(8,128)(2,1)S(1)}, bf16[1,160,160]{2,1,0:T(8,128)(2,1)}, u32[]{:S(2)}) %copy-start.1) | copy-done | bytes 51224
  1.5 7.5 %halo.1 = (bf16[3,192,176]{2,1,0:T(8,128)(2,1)S(1)}, bf16[3,192,176]{2,1,0:T(8,128)(2,1)S(1)}) custom-call(bf16[160,160]{1,0:T(8,128)(2,1)S(1)} %bitcast.11), custom_call_target="tpu_custom_call" | custom-call | tf_op jit(solution)/shard_map/halo/pallas_call | solution.py:420
  9.1 0.8 %copy.12.kernel1 = bf16[32,9]{1,0:T(8,128)(2,1)S(1)} copy(bf16[32,9]{0,1:T(8,128)(2,1)} %param.10) | data formatting | bytes 1152 | tf_op args[1]
  9.8 0.0 copy-start.2
  9.8 0.9 %copy-done.2 = bf16[160,256]{1,0:T(8,128)(2,1)S(1)} copy-done((bf16[160,256]{1,0:T(8,128)(2,1)S(1)}, bf16[160,256]{1,0:T(8,128)(2,1)}, u32[]{:S(2)}) %copy-start.2) | copy-done | bytes 81944
  10.7 0.0 copy-start.3
  10.7 0.7 copy-done.3
  11.5 0.0 copy-start.5
  11.5 0.7 copy-done.5
  12.1 0.0 copy-start.6
  12.1 0.7 copy-done.6
  12.8 17.2 %encode.1 = (bf16[160,5120]{1,0:T(8,128)(2,1)}, f32[2,5120,128]{2,1,0:T(8,128)S(1)}) custom-call(bf16[3,192,176]{2,1,0:T(8,128)(2,1)S(1)} %get-tuple-element.9.across, bf16[3,192,176]{2,1,0:T(8,128)(2,1)S(1)} %get-tuple-element.10.down, bf16[32,9]{1,0:T(8,128)(2,1)S(1)} %copy.12.kernel1, bf16[32,288]{1,0:T(8,128)(2,1)S(1)} %copy-done.3, ...), custom_call_target="tpu_custom_call" | custom-call | tf_op jit(solution)/shard_map/encode/pallas_call | solution.py:440
  30.6 0.0 copy-start
  30.6 1.3 %copy-done = f32[320,1024]{1,0:T(8,128)S(1)} copy-done((f32[320,1024]{1,0:T(8,128)S(1)}, f32[320,1024]{1,0:T(8,128)}, u32[]{:S(2)}) %copy-start) | copy-done | bytes 1310744
  31.9 0.0 copy-start.4
  31.9 0.7 copy-done.4
  32.6 39.9 %mesh.1 = (f32[8,128]{1,0:T(8,128)S(1)}, f32[8,128]{1,0:T(8,128)S(1)}) custom-call(s32[1]{0:T(128)} %bitcast.10.tissue, s32[2]{0:T(128)S(1)} %bitcast.12, f32[2,5120,128]{2,1,0:T(8,128)S(1)} %get-tuple-element.12.rowwise, f32[320,1024]{1,0:T(8,128)S(1)} %copy-done), custom_call_target="tpu_custom_call" | custom-call | tf_op jit(solution)/shard_map/mesh/pallas_call | solution.py:474
  72.5 0.6 copy.14
  73.2 0.5 slice_bitcast_fusion.1
  (1 shorter events, 0.0 us)
Async XLA Ops:
  0.6 0.9 %copy-start.1 = (bf16[1,160,160]{2,1,0:T(8,128)(2,1)S(1)}, bf16[1,160,160]{2,1,0:T(8,128)(2,1)}, u32[]{:S(2)}) copy-start(bf16[1,160,160]{2,1,0:T(8,128)(2,1)} %param.9) | copy-start | bytes 153604
  9.8 0.9 %copy-start.2 = (bf16[160,256]{1,0:T(8,128)(2,1)S(1)}, bf16[160,256]{1,0:T(8,128)(2,1)}, u32[]{:S(2)}) copy-start(bf16[160,256]{1,0:T(8,128)(2,1)} %constant.4.clone.first) | copy-start | bytes 245764
  10.7 0.7 %copy-start.3 = (bf16[32,288]{1,0:T(8,128)(2,1)S(1)}, bf16[32,288]{1,0:T(8,128)(2,1)}, u32[]{:S(2)}) copy-start(bf16[32,288]{1,0:T(8,128)(2,1)} %kernel2.1) | copy-start | bytes 55300
  11.5 0.7 copy-start.5
  12.1 0.7 copy-start.6
  30.6 1.3 %copy-start = (f32[320,1024]{1,0:T(8,128)S(1)}, f32[320,1024]{1,0:T(8,128)}, u32[]{:S(2)}) copy-start(f32[320,1024]{1,0:T(8,128)} %constant.5.clone.tables) | copy-start | bytes 3932164
  31.9 0.7 copy-start.4

commit v4 on v3

--- a/solution.py
+++ b/solution.py
@@ -212,7 +212,7 @@
             hidt[b, pl.ds(c0, lanes), :] = value[:, b : b + length].astype(BF)
         return carry
 
-    lax.fori_loop(0, wide // SPAN, first_layer, 0)
+    lax.fori_loop(0, wide // SPAN, first_layer, 0, unroll=wide // SPAN)
 
     def second_layer(blk, carry):
         c0 = pl.multiple_of(blk * cols, cols)

time: 74 us -> 73.1 us (0.988)
  Pallas kernels: 64.6 us -> 63.7 us
    pallas_call x1, Pallas kernels: 17.2 us -> 16.3 us  [body(): pl.pallas_call(encode_kernel, out_shape=(jax.ShapeDtypeStruct((length, le...]
where the time goes in v4:
time: 73.1 us; the launch traced here: 72.7 us
  Pallas kernels  63.7 us (87%)
  local copies, waits for them, and re-layouts  7.72 us (11%)
  between operations  1.33 us (2%)
    pallas_call x1, Pallas kernels, body(): pl.pallas_call(functools.partial(mesh_kernel, channels), out_shape=(jax.S...  39.9 us
    pallas_call x1, Pallas kernels, body(): pl.pallas_call(encode_kernel, out_shape=(jax.ShapeDtypeStruct((length, le...  16.3 us
    pallas_call x1, Pallas kernels, body(): pl.pallas_call(halo_kernel, out_shape=(frame, frame), in_specs=[vmem], ou...  7.53 us
    unnamed x16, local copies, waits for them, and re-layouts  7.21 us

profile of v4, /device:TPU:1, one launch (start us, length us, event | category | flops | bytes accessed | tf_op | source)
XLA Modules:
  0.0 72.7 jit_solution(9319645821149067567)
XLA Ops:
  0.6 0.0 copy-start.1
  0.6 0.9 %copy-done.1 = bf16[1,160,160]{2,1,0:T(8,128)(2,1)S(1)} copy-done((bf16[1,160,160]{2,1,0:T(8,128)(2,1)S(1)}, bf16[1,160,160]{2,1,0:T(8,128)(2,1)}, u32[]{:S(2)}) %copy-start.1) | copy-done | bytes 51224
  1.5 7.5 %halo.1 = (bf16[3,192,176]{2,1,0:T(8,128)(2,1)S(1)}, bf16[3,192,176]{2,1,0:T(8,128)(2,1)S(1)}) custom-call(bf16[160,160]{1,0:T(8,128)(2,1)S(1)} %bitcast.11), custom_call_target="tpu_custom_call" | custom-call | tf_op jit(solution)/shard_map/halo/pallas_call | solution.py:420
  9.1 0.8 %copy.12.kernel1 = bf16[32,9]{1,0:T(8,128)(2,1)S(1)} copy(bf16[32,9]{0,1:T(8,128)(2,1)} %param.10) | data formatting | bytes 1152 | tf_op args[1]
  9.8 0.0 copy-start.2
  9.8 0.9 %copy-done.2 = bf16[160,256]{1,0:T(8,128)(2,1)S(1)} copy-done((bf16[160,256]{1,0:T(8,128)(2,1)S(1)}, bf16[160,256]{1,0:T(8,128)(2,1)}, u32[]{:S(2)}) %copy-start.2) | copy-done | bytes 81944
  10.7 0.0 copy-start.3
  10.7 0.7 %copy-done.3 = bf16[32,288]{1,0:T(8,128)(2,1)S(1)} copy-done((bf16[32,288]{1,0:T(8,128)(2,1)S(1)}, bf16[32,288]{1,0:T(8,128)(2,1)}, u32[]{:S(2)}) %copy-start.3) | copy-done | bytes 18456
  11.5 0.0 copy-start.5
  11.5 0.7 copy-done.5
  12.1 0.0 copy-start.6
  12.1 0.7 copy-done.6
  12.8 16.3 %encode.1 = (bf16[160,5120]{1,0:T(8,128)(2,1)}, f32[2,5120,128]{2,1,0:T(8,128)S(1)}) custom-call(bf16[3,192,176]{2,1,0:T(8,128)(2,1)S(1)} %get-tuple-element.9.across, bf16[3,192,176]{2,1,0:T(8,128)(2,1)S(1)} %get-tuple-element.10.down, bf16[32,9]{1,0:T(8,128)(2,1)S(1)} %copy.12.kernel1, bf16[32,288]{1,0:T(8,128)(2,1)S(1)} %copy-done.3, ...), custom_call_target="tpu_custom_call" | custom-call | tf_op jit(solution)/shard_map/encode/pallas_call | solution.py:440
  29.7 0.0 copy-start
  29.7 1.3 %copy-done = f32[320,1024]{1,0:T(8,128)S(1)} copy-done((f32[320,1024]{1,0:T(8,128)S(1)}, f32[320,1024]{1,0:T(8,128)}, u32[]{:S(2)}) %copy-start) | copy-done | bytes 1310744
  31.0 0.0 copy-start.4
  31.0 0.7 copy-done.4
  31.7 39.9 %mesh.1 = (f32[8,128]{1,0:T(8,128)S(1)}, f32[8,128]{1,0:T(8,128)S(1)}) custom-call(s32[1]{0:T(128)} %bitcast.10.tissue, s32[2]{0:T(128)S(1)} %bitcast.12, f32[2,5120,128]{2,1,0:T(8,128)S(1)} %get-tuple-element.12.rowwise, f32[320,1024]{1,0:T(8,128)S(1)} %copy-done), custom_call_target="tpu_custom_call" | custom-call | tf_op jit(solution)/shard_map/mesh/pallas_call | solution.py:474
  71.6 0.6 copy.14
  72.2 0.5 slice_bitcast_fusion.1
  (1 shorter events, 0.0 us)
Async XLA Ops:
  0.6 0.9 %copy-start.1 = (bf16[1,160,160]{2,1,0:T(8,128)(2,1)S(1)}, bf16[1,160,160]{2,1,0:T(8,128)(2,1)}, u32[]{:S(2)}) copy-start(bf16[1,160,160]{2,1,0:T(8,128)(2,1)} %param.9) | copy-start | bytes 153604
  9.8 0.9 %copy-start.2 = (bf16[160,256]{1,0:T(8,128)(2,1)S(1)}, bf16[160,256]{1,0:T(8,128)(2,1)}, u32[]{:S(2)}) copy-start(bf16[160,256]{1,0:T(8,128)(2,1)} %constant.4.clone.first) | copy-start | bytes 245764
  10.7 0.7 %copy-start.3 = (bf16[32,288]{1,0:T(8,128)(2,1)S(1)}, bf16[32,288]{1,0:T(8,128)(2,1)}, u32[]{:S(2)}) copy-start(bf16[32,288]{1,0:T(8,128)(2,1)} %kernel2.1) | copy-start | bytes 55300
  11.5 0.7 copy-start.5
  12.1 0.7 copy-start.6
  29.7 1.3 %copy-start = (f32[320,1024]{1,0:T(8,128)S(1)}, f32[320,1024]{1,0:T(8,128)}, u32[]{:S(2)}) copy-start(f32[320,1024]{1,0:T(8,128)} %constant.5.clone.tables) | copy-start | bytes 3932164
  31.0 0.7 copy-start.4

commit v5 on v4

--- a/solution.py
+++ b/solution.py
@@ -227,7 +227,7 @@
         rowwise[1, pl.ds(c0, cols), :] = pair[:, HALF:]
         return carry
 
-    lax.fori_loop(0, length * channels // cols, second_layer, 0, unroll=4)
+    lax.fori_loop(0, length * channels // cols, second_layer, 0, unroll=10)
 
 
 def mesh_kernel(

time: 73.1 us -> 76.2 us (1.042)
  Pallas kernels: 63.7 us -> 66.8 us
    pallas_call x1, Pallas kernels: 16.3 us -> 19.4 us  [body(): pl.pallas_call(encode_kernel, out_shape=(jax.ShapeDtypeStruct((length, le...]
where the time goes in v5:
time: 76.2 us; the launch traced here: 75.9 us
  Pallas kernels  66.8 us (88%)
  local copies, waits for them, and re-layouts  7.72 us (10%)
  between operations  1.33 us (2%)
    pallas_call x1, Pallas kernels, body(): pl.pallas_call(functools.partial(mesh_kernel, channels), out_shape=(jax.S...  39.9 us
    pallas_call x1, Pallas kernels, body(): pl.pallas_call(encode_kernel, out_shape=(jax.ShapeDtypeStruct((length, le...  19.4 us
    pallas_call x1, Pallas kernels, body(): pl.pallas_call(halo_kernel, out_shape=(frame, frame), in_specs=[vmem], ou...  7.53 us
    unnamed x16, local copies, waits for them, and re-layouts  7.21 us

profile of v5, /device:TPU:1, one launch (start us, length us, event | category | flops | bytes accessed | tf_op | source)
XLA Modules:
  0.0 75.9 jit_solution(7474928197318745628)
XLA Ops:
  0.6 0.0 copy-start.1
  0.6 0.9 %copy-done.1 = bf16[1,160,160]{2,1,0:T(8,128)(2,1)S(1)} copy-done((bf16[1,160,160]{2,1,0:T(8,128)(2,1)S(1)}, bf16[1,160,160]{2,1,0:T(8,128)(2,1)}, u32[]{:S(2)}) %copy-start.1) | copy-done | bytes 51224
  1.5 7.5 %halo.1 = (bf16[3,192,176]{2,1,0:T(8,128)(2,1)S(1)}, bf16[3,192,176]{2,1,0:T(8,128)(2,1)S(1)}) custom-call(bf16[160,160]{1,0:T(8,128)(2,1)S(1)} %bitcast.11), custom_call_target="tpu_custom_call" | custom-call | tf_op jit(solution)/shard_map/halo/pallas_call | solution.py:420
  9.1 0.8 %copy.12.kernel1 = bf16[32,9]{1,0:T(8,128)(2,1)S(1)} copy(bf16[32,9]{0,1:T(8,128)(2,1)} %param.10) | data formatting | bytes 1152 | tf_op args[1]
  9.8 0.0 copy-start.2
  9.8 0.9 %copy-done.2 = bf16[160,256]{1,0:T(8,128)(2,1)S(1)} copy-done((bf16[160,256]{1,0:T(8,128)(2,1)S(1)}, bf16[160,256]{1,0:T(8,128)(2,1)}, u32[]{:S(2)}) %copy-start.2) | copy-done | bytes 81944
  10.7 0.0 copy-start.3
  10.7 0.7 copy-done.3
  11.5 0.0 copy-start.5
  11.5 0.7 copy-done.5
  12.1 0.0 copy-start.6
  12.1 0.7 copy-done.6
  12.8 19.4 %encode.1 = (bf16[160,5120]{1,0:T(8,128)(2,1)}, f32[2,5120,128]{2,1,0:T(8,128)S(1)}) custom-call(bf16[3,192,176]{2,1,0:T(8,128)(2,1)S(1)} %get-tuple-element.9.across, bf16[3,192,176]{2,1,0:T(8,128)(2,1)S(1)} %get-tuple-element.10.down, bf16[32,9]{1,0:T(8,128)(2,1)S(1)} %copy.12.kernel1, bf16[32,288]{1,0:T(8,128)(2,1)S(1)} %copy-done.3, ...), custom_call_target="tpu_custom_call" | custom-call | tf_op jit(solution)/shard_map/encode/pallas_call | solution.py:440
  32.8 0.0 copy-start
  32.8 1.3 %copy-done = f32[320,1024]{1,0:T(8,128)S(1)} copy-done((f32[320,1024]{1,0:T(8,128)S(1)}, f32[320,1024]{1,0:T(8,128)}, u32[]{:S(2)}) %copy-start) | copy-done | bytes 1310744
  34.1 0.0 copy-start.4
  34.1 0.7 copy-done.4
  34.8 39.9 %mesh.1 = (f32[8,128]{1,0:T(8,128)S(1)}, f32[8,128]{1,0:T(8,128)S(1)}) custom-call(s32[1]{0:T(128)} %bitcast.10.tissue, s32[2]{0:T(128)S(1)} %bitcast.12, f32[2,5120,128]{2,1,0:T(8,128)S(1)} %get-tuple-element.12.rowwise, f32[320,1024]{1,0:T(8,128)S(1)} %copy-done), custom_call_target="tpu_custom_call" | custom-call | tf_op jit(solution)/shard_map/mesh/pallas_call | solution.py:474
  74.7 0.6 copy.14
  75.4 0.5 slice_bitcast_fusion.1
  (1 shorter events, 0.0 us)
Async XLA Ops:
  0.6 0.9 %copy-start.1 = (bf16[1,160,160]{2,1,0:T(8,128)(2,1)S(1)}, bf16[1,160,160]{2,1,0:T(8,128)(2,1)}, u32[]{:S(2)}) copy-start(bf16[1,160,160]{2,1,0:T(8,128)(2,1)} %param.9) | copy-start | bytes 153604
  9.8 0.9 %copy-start.2 = (bf16[160,256]{1,0:T(8,128)(2,1)S(1)}, bf16[160,256]{1,0:T(8,128)(2,1)}, u32[]{:S(2)}) copy-start(bf16[160,256]{1,0:T(8,128)(2,1)} %constant.4.clone.first) | copy-start | bytes 245764
  10.7 0.7 copy-start.3
  11.5 0.7 copy-start.5
  12.1 0.7 copy-start.6
  32.8 1.3 %copy-start = (f32[320,1024]{1,0:T(8,128)S(1)}, f32[320,1024]{1,0:T(8,128)}, u32[]{:S(2)}) copy-start(f32[320,1024]{1,0:T(8,128)} %constant.5.clone.tables) | copy-start | bytes 3932164
  34.1 0.7 copy-start.4
